TPU v7x, 256 devices: a whole 4x4x8 slice. The times are simulated.
256 devices in a mesh: band: 8 (over y, core), fft: 32 (over x, z).
Axes of the slice: x: 4, y: 4, z: 8, core: 2. Of those that a mesh axis runs over, the one named last changes fastest.
Arguments:
- current: float32 [2, 64, 98304], P(None, 'band', 'fft'), may hold values from -100 to 100
- h_current: float32 [2, 64, 98304], P(None, 'band', 'fft'), may hold values from -100 to 100
- previous: float32 [2, 64, 98304], P(None, 'band', 'fft'), may hold values from -100 to 100
- h_previous: float32 [2, 64, 98304], P(None, 'band', 'fft'), may hold values from -100 to 100
- eigen_values: float32 [64], P('band'), may hold values from -1 to 3
- potential: float32 [96, 96, 96], P('fft'), may hold values from -3 to 1
- stick_cols: int32 [4096], replicated, may hold values from -1 to 9215, as said below
- g_map: int32 [98304], P('fft'), may hold values from -1 to 12287, as said below
Outputs:
- h_residual: float32 [2, 64, 98304], P(None, 'band', 'fft')
- correlation_matrix: float32 [2, 192, 192], P(None, 'band', 'fft')
- hamiltonian_matrix: float32 [2, 192, 192], P(None, 'band', 'fft')
Inputs may be any that keep to these rules, and one draw needn't show every extreme that they name: `stick_cols`: each grid column x * 96 + y whose signed frequencies satisfy x*x + y*y <= 24^2 is named by exactly one slot and all other slots are -1; fft device d owns slots d * 128 to (d + 1) * 128 - 1, its named slots are its last ones, and the numbers of named slots of two devices differ by at most one. `g_map`: the live entries of an fft device come first among its 3072 entries and name each G-vector of its named sticks once: local slot s and grid index z such that the signed frequencies of the stick's column and of z satisfy x*x + y*y + z*z <= 24^2; all other entries are -1.
All inputs are finite; a program needn't handle non-finite values.
Results may differ from a plain program's by a relative error of at most 0.00005.
Values sent between devices are 32-bit elements; how exact they have to be, the bound alone decides.
A program may use at most 64 MiB of HBM per device.

v0:
```python
import math

import jax
import jax.numpy as jnp
from jax import lax
from jax.sharding import PartitionSpec as P

EXACT = lax.Precision.HIGHEST


def signed_index(values, length):
    return jnp.where(values >= length // 2, values - length, values)


def dft_table(length, direction_sign):
    positions = jnp.arange(length, dtype=jnp.int32)
    wrapped = positions[:, None] * positions[None, :] % length
    angles = wrapped.astype(jnp.float32) * (2.0 * math.pi / length)
    cosine = jnp.cos(angles)
    sine_part = direction_sign * jnp.sin(angles)
    upper_rows = jnp.stack([cosine, sine_part], axis=1)
    lower_rows = jnp.stack([-sine_part, cosine], axis=1)
    return jnp.stack([upper_rows, lower_rows], axis=0)


def along_trailing(field, matrix):
    shape_now = field.shape
    flat_field = field.reshape(-1, matrix.shape[0])
    return jnp.dot(flat_field, matrix, precision=EXACT, preferred_element_type=jnp.float32).reshape(
        shape_now
    )


def gram_terms(row_block, col_block, h_col_block, gram_scale):
    left_side = jnp.concatenate([row_block[0], row_block[1]], axis=1)
    right_side = jnp.concatenate(
        [
            jnp.concatenate([col_block[0], col_block[1]], axis=1),
            jnp.concatenate([col_block[1], -col_block[0]], axis=1),
            jnp.concatenate([h_col_block[0], h_col_block[1]], axis=1),
            jnp.concatenate([h_col_block[1], -h_col_block[0]], axis=1),
        ],
        axis=0,
    )
    product = lax.dot_general(
        left_side,
        right_side,
        (((1,), (1,)), ((), ())),
        precision=EXACT,
        preferred_element_type=jnp.float32,
    )
    order = col_block.shape[1]
    return jnp.transpose(product.reshape(row_block.shape[1], 4, order), (1, 0, 2)) * gram_scale


def local(current, h_current, previous, h_previous, eigen_values, potential, stick_cols, g_map):
    fft_count = lax.axis_size("fft")
    band_count = lax.axis_size("band")
    grid_length = potential.shape[1]
    plane_count = grid_length * grid_length
    slot_count = stick_cols.shape[0] // fft_count
    stick_total = stick_cols.shape[0]
    band_local = current.shape[1]
    g_local = g_map.shape[0]
    local_cols = lax.dynamic_slice_in_dim(
        stick_cols, lax.axis_index("fft") * slot_count, slot_count
    )
    live_mask = g_map >= 0
    safe_map = jnp.where(live_mask, g_map, 0)
    slot_of = safe_map // grid_length
    z_index = safe_map % grid_length
    column = jnp.sum(
        jnp.where(
            slot_of[:, None] == jnp.arange(slot_count, dtype=jnp.int32)[None, :],
            local_cols[None, :],
            0,
        ),
        axis=1,
    )
    x_freq = signed_index(column // grid_length, grid_length)
    y_freq = signed_index(column % grid_length, grid_length)
    z_freq = signed_index(z_index, grid_length)
    norm_sq = x_freq * x_freq + y_freq * y_freq + z_freq * z_freq
    kinetic = jnp.where(live_mask, 64.0 * norm_sq.astype(jnp.float32) / float(plane_count), 0.0)
    residual = jnp.where(
        live_mask, (h_current - eigen_values[None, :, None] * current) / (1.0 + kinetic), 0.0
    )
    stick_cells = grid_length * slot_count
    stick_index = jnp.where(live_mask, z_index * slot_count + slot_of, stick_cells)
    slot_inverse = (
        jnp.full((stick_cells,), g_local, jnp.int32)
        .at[stick_index]
        .set(jnp.arange(g_local, dtype=jnp.int32), mode="drop")
    )
    residual_rows = jnp.transpose(residual, (2, 0, 1))
    residual_rows = jnp.concatenate(
        [residual_rows, jnp.zeros((1, 2, band_local), jnp.float32)], axis=0
    )
    sticks = jnp.take(residual_rows, slot_inverse, axis=0).reshape(
        grid_length, slot_count, 2, band_local
    )
    toward = dft_table(grid_length, 1.0)
    backward = dft_table(grid_length, -1.0)
    toward_flat = toward.reshape(2 * grid_length, 2 * grid_length)
    backward_flat = backward.reshape(2 * grid_length, 2 * grid_length)
    spectra = jnp.einsum(
        "zscb,czdk->dbks", sticks, toward, precision=EXACT, preferred_element_type=jnp.float32
    )
    place_index = jnp.where(stick_cols >= 0, stick_cols, plane_count)
    plane_inverse = (
        jnp.full((plane_count,), stick_total, jnp.int32)
        .at[place_index]
        .set(jnp.arange(stick_total, dtype=jnp.int32), mode="drop")
    )
    safe_place = jnp.maximum(stick_cols, 0)
    stick_live = (stick_cols >= 0).astype(jnp.float32)
    potential_xy = jnp.transpose(potential, (0, 1, 2))[None, :, :, None, :]
    stick_piece = lax.all_to_all(spectra, "fft", split_axis=2, concat_axis=3, tiled=True)
    item_count = stick_piece.shape[1]
    plane_depth = stick_piece.shape[2]
    width = 2 * item_count * plane_depth
    piece_rows = jnp.transpose(stick_piece, (3, 0, 1, 2)).reshape(stick_total, width)
    piece_rows = jnp.concatenate([piece_rows, jnp.zeros((1, width), jnp.float32)], axis=0)
    grid_rows = jnp.take(piece_rows, plane_inverse, axis=0)
    grid_rows = grid_rows.reshape(grid_length, grid_length, 2, item_count, plane_depth)
    planes = jnp.transpose(grid_rows, (3, 4, 0, 2, 1))
    planes = along_trailing(
        planes.reshape(item_count, plane_depth, grid_length, 2 * grid_length), toward_flat
    )
    planes = planes.reshape(item_count, plane_depth, grid_length, 2, grid_length)
    planes = jnp.einsum(
        "nzxcy,cxdk->nzkdy", planes, toward, precision=EXACT, preferred_element_type=jnp.float32
    )
    planes = planes * potential_xy
    planes = jnp.einsum(
        "nzxcy,cxdk->nzkdy", planes, backward, precision=EXACT, preferred_element_type=jnp.float32
    )
    planes = along_trailing(
        planes.reshape(item_count, plane_depth, grid_length, 2 * grid_length), backward_flat
    )
    planes = planes.reshape(item_count, plane_depth, grid_length, 2, grid_length)
    cell_rows = jnp.transpose(planes, (2, 4, 3, 0, 1)).reshape(plane_count, width)
    picked = jnp.take(cell_rows, safe_place, axis=0) * stick_live[:, None]
    picked = jnp.transpose(picked.reshape(stick_total, 2, item_count, plane_depth), (1, 2, 3, 0))
    returned = lax.all_to_all(picked, "fft", split_axis=3, concat_axis=2, tiled=True)
    coeff_rows = jnp.einsum(
        "cbzs,czdk->ksdb", returned, backward, precision=EXACT, preferred_element_type=jnp.float32
    )
    coeff_rows = coeff_rows.reshape(stick_cells, 2, band_local)
    picked_rows = jnp.take(coeff_rows, jnp.where(live_mask, stick_index, 0), axis=0)
    potential_term = jnp.transpose(picked_rows, (1, 2, 0)) / float(plane_count * grid_length)
    h_residual = jnp.where(live_mask, kinetic * residual + potential_term, 0.0)
    basis = jnp.stack(
        [jnp.where(live_mask, current, 0.0), residual, jnp.where(live_mask, previous, 0.0)], axis=1
    )
    h_basis = jnp.stack(
        [jnp.where(live_mask, h_current, 0.0), h_residual, jnp.where(live_mask, h_previous, 0.0)],
        axis=1,
    )
    order = 3 * band_local * band_count
    row_share = order // band_count
    col_share = order // fft_count
    gram_scale = 8.0 / float(grid_length**3)
    basis_all, h_basis_all = (
        lax.all_to_all(basis, "band", split_axis=3, concat_axis=2, tiled=True),
        lax.all_to_all(h_basis, "band", split_axis=3, concat_axis=2, tiled=True),
    )
    g_width = basis_all.shape[3]
    basis_all = basis_all.reshape(2, order, g_width)
    h_basis_all = h_basis_all.reshape(2, order, g_width)
    partial_value = gram_terms(basis_all, basis_all, h_basis_all, gram_scale)
    summed = lax.psum(partial_value, ("band", "fft"))
    summed = lax.dynamic_slice_in_dim(summed, lax.axis_index("band") * row_share, row_share, 1)
    summed = lax.dynamic_slice_in_dim(summed, lax.axis_index("fft") * col_share, col_share, 2)
    return (h_residual, summed[0:2], summed[2:4])


def solution(mesh):
    in_specs = (
        P(None, "band", "fft"),
        P(None, "band", "fft"),
        P(None, "band", "fft"),
        P(None, "band", "fft"),
        P("band"),
        P("fft", None, None),
        P(),
        P("fft"),
    )
    out_specs = (P(None, "band", "fft"), P(None, "band", "fft"), P(None, "band", "fft"))
    return jax.shard_map(local, mesh=mesh, in_specs=in_specs, out_specs=out_specs, check_vma=False)
```

profile of v0, /device:TPU:4, one launch (start us, length us, event | category | flops | bytes accessed | tf_op | source)
XLA Modules:
  0.0 767.9 jit_solution(7884899939499815406)
XLA Ops:
  9.2 11.8 %scatter_custom_fusion.1 = s32[12288]{0:T(1024)S(1)} fusion(s32[3072]{0:T(1024)S(1)} %get-tuple-element.47, s32[3072]{0:T(1024)S(1)} %iota.47, s32[]{:T(128)} %constant.154.clone.1), kind=kCustom, calls=%fused_computation.90 | custom fusion | bytes 49156 | tf_op jit(solution)/shard_map/scatter | solution.py:93
  36.6 84.2 %gather_fusion = f32[12288,2,8]{2,1,0:T(2,128)} fusion(f32[3073,2,8]{2,1,0:T(2,128)S(1)} %concatenate.22.clone, s32[12288]{0:T(1024)} %fusion.53), kind=kCustom, calls=%fused_computation | custom fusion | bytes 1622016 | tf_op jit(solution)/shard_map/jit(_take)/gather | solution.py:99
  120.8 9.9 %copy.268 = f32[96,128,2,8]{1,0,2,3:T(8,128)S(1)} copy(f32[96,128,2,8]{3,2,1,0:T(2,128)} %bitcast.158) | data formatting | bytes 1572864 | tf_op jit(solution)/shard_map/jit(_take)/gather | solution.py:99
  133.0 11.6 %all-to-all-start = ((f32[2,8,96,128]{3,1,0,2:T(8,128)}), f32[2,8,96,128]{3,1,0,2:T(8,128)S(1)}, u32[]{:S(2)}, u32[]{:S(2)}) async-start(f32[2,8,96,128]{3,1,0,2:T(8,128)} %copy.269), calls=%async_computation | async-start | bytes 1572864 | tf_op jit(solution)/shard_map/all_to_all | solution.py:118
  145.2 15.5 %scatter_custom_fusion = s32[9216]{0:T(1024)S(1)} fusion(s32[4096]{0:T(1024)S(1)} %get-tuple-element.45, s32[4096]{0:T(1024)S(1)} %iota.46, s32[]{:T(128)} %constant.141.clone.1), kind=kCustom, calls=%fused_computation.101 | custom fusion | bytes 36868 | tf_op jit(solution)/shard_map/scatter | solution.py:113
  170.5 31.4 %gather_fusion.1 = f32[9216,48]{1,0:T(8,128)} fusion(f32[4097,48]{1,0:T(8,128)S(1)} %concatenate.23, s32[9216]{0:T(1024)S(1)} %fusion.54), kind=kCustom, calls=%fused_computation.1 | custom fusion | bytes 3575808 | tf_op jit(solution)/shard_map/jit(_take)/gather | solution.py:124
  224.9 6.3 convolution_bitcast_fusion
  238.6 13.1 %gather_fusion.2 = f32[4096,48]{1,0:T(8,128)S(1)} fusion(f32[9216,48]{1,0:T(8,128)} %copy.285, s32[4096]{0:T(1024)S(1)} %copy-done.6), kind=kCustom, calls=%fused_computation.2 | custom fusion | bytes 1589248 | tf_op jit(solution)/shard_map/jit(_take)/gather | solution.py:143
  253.0 15.2 %copy.287 = f32[2,8,3,4096]{1,0,2,3:T(2,128)} copy(f32[2,8,3,4096]{3,2,1,0:T(4,128)S(1)} %multiply_bitcast_fusion) | data formatting | bytes 1572864 | tf_op jit(solution)/shard_map/transpose | solution.py:144
  268.1 18.7 %reshape.249 = f32[32,1,6144]{2,1,0:T(1,128)S(1)} reshape(f32[4096,3,2,8]{3,2,1,0:T(2,128)} %bitcast.156) | data formatting | bytes 1572864
  286.8 27.7 %all_to_all.66 = f32[32,1,6144]{2,1,0:T(1,128)S(1)} all-to-all(f32[32,1,6144]{2,1,0:T(1,128)S(1)} %reshape.249), channel_id=1, replica_groups=mesh['band'=8,'fft'=32] {'fft'}, dimensions={0} | all-to-all | bytes 1572864 | tf_op jit(solution)/shard_map/all_to_all | solution.py:145
  317.6 20.9 %reshape.250 = f32[4096,3,2,8]{3,2,1,0:T(2,128)} reshape(f32[32,6144]{1,0:T(8,128)S(1)} %reduce) | data formatting | bytes 1572864
  338.5 14.3 %copy.326 = f32[2,8,3,32,128]{4,1,2,3,0:T(8,128)S(1)} copy(f32[2,8,3,32,128]{1,0,2,4,3:T(2,128)} %bitcast.157) | data formatting | bytes 1572864 | tf_op jit(solution)/shard_map/all_to_all | solution.py:145
  353.7 8.4 %copy.327 = f32[96,128,2,8]{3,2,1,0:T(2,128)} copy(f32[96,128,2,8]{1,0,3,2:T(8,128)S(1)} %convolution_bitcast_fusion.1) | data formatting | bytes 1572864 | tf_op jit(solution)/shard_map/reshape | solution.py:149
  362.1 14.6 %gather_fusion.3 = f32[3072,2,8]{2,1,0:T(2,128)S(1)} fusion(f32[12288,2,8]{2,1,0:T(2,128)} %bitcast.163, s32[3072]{0:T(1024)S(1)} %copy-done.9), kind=kCustom, calls=%fused_computation.3 | custom fusion | bytes 405504 | tf_op jit(solution)/shard_map/jit(_take)/gather | solution.py:150
  381.4 9.1 %copy.294 = f32[2,3,8,3072]{2,0,1,3:T(2,128)} copy(f32[2,3,8,3072]{3,2,0,1:T(8,128)S(1)} %get-tuple-element.51) | data formatting | bytes 1179648 | tf_op jit(solution)/shard_map/stack | solution.py:153
  390.6 17.6 %reshape.253 = f32[8,1,18432]{2,1,0:T(1,128)} reshape(f32[3072,3,2,8]{3,2,1,0:T(2,128)} %bitcast.159) | data formatting | bytes 1179648
  412.9 9.1 %copy.298 = f32[2,3,8,3072]{2,0,1,3:T(2,128)} copy(f32[2,3,8,3072]{3,2,0,1:T(8,128)S(1)} %get-tuple-element.52) | data formatting | bytes 1179648 | tf_op jit(solution)/shard_map/stack | solution.py:156
  422.1 17.6 %reshape.251 = f32[8,1,18432]{2,1,0:T(1,128)} reshape(f32[3072,3,2,8]{3,2,1,0:T(2,128)} %bitcast.160) | data formatting | bytes 1179648
  446.6 18.0 %reshape.254 = f32[3072,3,2,8]{3,2,1,0:T(2,128)} reshape(f32[8,18432]{1,0:T(8,128)S(1)} %reduce.2) | data formatting | bytes 1179648
  464.7 8.0 %copy.328 = f32[2,3,8,8,384]{4,3,2,1,0:T(8,128)S(1)} copy(f32[2,3,8,8,384]{2,0,1,4,3:T(2,128)} %bitcast.161) | data formatting | bytes 1179648 | tf_op jit(solution)/shard_map/all_to_all | solution.py:165
  474.9 18.0 %reshape.252 = f32[3072,3,2,8]{3,2,1,0:T(2,128)} reshape(f32[8,18432]{1,0:T(8,128)S(1)} %reduce.1) | data formatting | bytes 1179648
  492.9 8.1 %copy.329 = f32[2,3,8,8,384]{4,3,2,1,0:T(8,128)S(1)} copy(f32[2,3,8,8,384]{2,0,1,4,3:T(2,128)} %bitcast.162) | data formatting | bytes 1179648 | tf_op jit(solution)/shard_map/all_to_all | solution.py:166
  505.7 253.4 %all-reduce.4.cloned.1.call-done = f32[4,192,192]{1,0,2:T(4,128)} async-done(((f32[4,192,192]{1,0,2:T(4,128)}), f32[4,192,192]{1,0,2:T(4,128)}) %all-reduce.4.cloned.1.call-update) | async-done | bytes 589840 | tf_op jit(solution)/shard_map/psum | solution.py:172
  (100 shorter events, 90.1 us)
Async XLA Ops:
  120.8 9.9 %copy-start.3 = (f32[96,1,96]{0,2,1:T(8,128)S(1)}, f32[96,1,96]{0,2,1:T(8,128)}, u32[]{:S(2)}) copy-start(f32[96,1,96]{0,2,1:T(8,128)} %fusion.58) | copy-start | bytes 110596
  120.8 10.0 %copy-start.7 = (pred[96,128]{1,0:T(8,128)(4,1)S(1)}, pred[96,128]{1,0:T(8,128)(4,1)}, u32[]{:S(2)}) copy-start(pred[96,128]{1,0:T(8,128)(4,1)} %and_bitcast_fusion) | copy-start | bytes 36868
  130.8 13.8 %copy-start.5 = (s32[4096]{0:T(1024)S(1)}, s32[4096]{0:T(1024)}, u32[]{:S(2)}) copy-start(s32[4096]{0:T(1024)} %param.14) | copy-start | bytes 49156
  133.0 32.4 %all-to-all-start = ((f32[2,8,96,128]{3,1,0,2:T(8,128)}), f32[2,8,96,128]{3,1,0,2:T(8,128)S(1)}, u32[]{:S(2)}, u32[]{:S(2)}) async-start(f32[2,8,96,128]{3,1,0,2:T(8,128)} %copy.269), calls=%async_computation | async-start | bytes 1572864 | tf_op jit(solution)/shard_map/all_to_all | solution.py:118
  205.6 2.4 copy-start.8
  218.1 2.3 copy-start
  218.1 2.3 copy-start.4
  234.0 4.6 copy-start.6
  338.5 14.3 %copy-start.2 = (f32[2,96,2,96,1]{1,3,2,0,4:T(8,128)S(1)}, f32[2,96,2,96,1]{1,3,2,0,4:T(8,128)}, u32[]{:S(2)}) copy-start(f32[2,96,2,96,1]{1,3,2,0,4:T(8,128)} %get-tuple-element.35) | copy-start | bytes 442372
  353.7 8.4 %copy-start.9 = (s32[3072]{0:T(1024)S(1)}, s32[3072]{0:T(1024)}, u32[]{:S(2)}) copy-start(s32[3072]{0:T(1024)} %get-tuple-element.46) | copy-start | bytes 36868
  380.0 10.5 %copy-start.1 = (f32[2,8,3072]{2,1,0:T(8,128)}, f32[2,8,3072]{2,1,0:T(8,128)S(1)}, u32[]{:S(2)}) copy-start(f32[2,8,3072]{2,1,0:T(8,128)S(1)} %fusion.39) | copy-start | bytes 589828
  408.2 31.5 %all-to-all-start.2 = ((f32[8,1,18432]{2,1,0:T(1,128)}), f32[8,1,18432]{2,1,0:T(1,128)S(1)}, u32[]{:S(2)}, u32[]{:S(2)}) async-start(f32[8,1,18432]{2,1,0:T(1,128)} %reshape.253), calls=%async_computation.2 | async-start | bytes 1179648 | tf_op jit(solution)/shard_map/all_to_all | solution.py:165
  439.7 33.1 %all-to-all-start.3 = ((f32[8,1,18432]{2,1,0:T(1,128)}), f32[8,1,18432]{2,1,0:T(1,128)S(1)}, u32[]{:S(2)}, u32[]{:S(2)}) async-start(f32[8,1,18432]{2,1,0:T(1,128)} %reshape.251), calls=%async_computation.3 | async-start | bytes 1179648 | tf_op jit(solution)/shard_map/all_to_all | solution.py:166
  444.5 314.6 %all-reduce.4.cloned.1.call-start = ((), (), s32[]{:S(2)}) async-start(), calls=%async_computation.4 | async-start | bytes 1572864 | tf_op jit(solution)/shard_map/psum | solution.py:172
Sparse Core Ops, SparseCore 0:
  505.8 253.2 all-reduce.3
where the time goes:
time: 777 us; the launch traced here: 768 us
  local copies, waits for them, and re-layouts  404 us (52%)
  waiting for transfers between devices  256 us (33%)
  blocking collectives  27.7 us (4%)
  other arithmetic  22.8 us (3%)
  matrix products  21.2 us (3%)
  starting transfers between devices  21.1 us (3%)
  between operations  15.1 us (2%)
    psum x1, waiting for transfers between devices, local(): summed = lax.psum(partial_value, ('band', 'fft'))  253 us
    unnamed x27, local copies, waits for them, and re-layouts  114 us
    gather x2, local copies, waits for them, and re-layouts, local(): jnp.take(residual_rows, slot_inverse, axis=0)  94.1 us
    gather x3, local copies, waits for them, and re-layouts, local(): grid_rows = jnp.take(piece_rows, plane_inverse, axis=0)  37.5 us
    all_to_all x1, blocking collectives, local(): lax.all_to_all(picked, 'fft', split_axis=3, concat_axis=2, tiled=True)  27.7 us
    gather x2, local copies, waits for them, and re-layouts, local(): jnp.take(coeff_rows, jnp.where(live_mask, stick_index, 0), axis=0)  17.1 us
  transfers between devices with their start and end apart: 4, of which 2 were waited for; matrix products, arithmetic and copies ran while one was open for 10% of the time, Pallas kernels for 0%

commit v1 on v0

v1 whole, which is shorter than its diff:
```python
import functools
import math

import jax
import jax.numpy as jnp
import ml_dtypes
import numpy as np
from jax import lax
from jax.experimental import pallas as pl
from jax.experimental.pallas import tpu as pltpu
from jax.sharding import PartitionSpec as P

L = 96
CUT = 24
F32 = jnp.float32
BF16 = jnp.bfloat16
NF = 32
NBD = 8
GT = 24
NPAIR = 25
MESH = pl.DeviceIdType.MESH
VM = pl.BlockSpec(memory_space=pltpu.VMEM)
SM = pl.BlockSpec(memory_space=pltpu.SMEM)


def split_np(table):
    high = table.astype(ml_dtypes.bfloat16)
    low = (table - high.astype(np.float64)).astype(ml_dtypes.bfloat16)
    return high, low


def tables():
    zout = (np.arange(NF)[None, :] * 3 + np.arange(3)[:, None]).reshape(-1)
    wz = np.zeros((2, 2, L, 2, 32))
    for par in range(2):
        zi = 2 * np.arange(32) + par
        ok = zi <= 2 * CUT
        ang = 2 * math.pi / L * ((zout[:, None] * (zi - CUT)[None, :]) % L)
        c, s = np.cos(ang) * ok, np.sin(ang) * ok
        wz[par, 0, :, 0], wz[par, 0, :, 1] = c, -s
        wz[par, 1, :, 0], wz[par, 1, :, 1] = s, c
    zh, zl = split_np(wz.reshape(384, 64))
    wz = np.concatenate([zh, zh, zl], axis=1)
    n = np.arange(L)
    k = np.arange(49) - CUT
    ang = 2 * math.pi / L * ((k[:, None] * n[None, :]) % L)
    c, s = np.cos(ang), np.sin(ang)
    wy = np.zeros((2, 64, 2, 128))
    wy[0, :49, 0, :L], wy[0, :49, 1, :L] = c, s
    wy[1, :49, 0, :L], wy[1, :49, 1, :L] = -s, c
    yh, yl = split_np(wy.reshape(128, 256))
    wy = np.concatenate([yh, yh, yl], axis=0)
    wx = np.zeros((2, L, 2, 56))
    wx[0, :, 0, :49], wx[0, :, 1, :49] = c.T, -s.T
    wx[1, :, 0, :49], wx[1, :, 1, :49] = s.T, c.T
    xh, xl = split_np(wx.reshape(192, 112))
    wxa = np.concatenate([xh, xh], axis=1)
    wxb = xl
    vx = np.zeros((2, 56, 2, L))
    vx[0, :49, 0], vx[0, :49, 1] = c, s
    vx[1, :49, 0], vx[1, :49, 1] = -s, c
    vh, vl = split_np(vx.reshape(112, 192))
    vx = np.concatenate([vh, vl], axis=0)
    vy = np.zeros((2, 128, 2, 64))
    vy[0, :L, 0, :49], vy[0, :L, 1, :49] = c.T, -s.T
    vy[1, :L, 0, :49], vy[1, :L, 1, :49] = s.T, c.T
    vyh, vyl = split_np(vy.reshape(256, 128))
    vy = np.concatenate([vyh, vyl], axis=1)
    vz = np.zeros((2, 64, L))
    ang = 2 * math.pi / L * ((k[:, None] * zout[None, :]) % L)
    vz[0, :49], vz[1, :49] = np.cos(ang), np.sin(ang)
    zbh, zbl = split_np(vz.reshape(128, L))
    vza = np.concatenate([zbh, zbh], axis=1)
    return dict(wz=wz, wy=wy, wxa=wxa, wxb=wxb, vx=vx, vy=vy, vza=vza, vzb=zbl)


def dot(a, b):
    return jnp.dot(a, b, preferred_element_type=F32)


def dot_nt(a, b):
    return lax.dot_general(a, b, (((1,), (1,)), ((), ())), preferred_element_type=F32)


def halves(x):
    hi = x.astype(BF16)
    return hi, (x - hi.astype(F32)).astype(BF16)


def low_lanes(shape):
    return lax.broadcasted_iota(jnp.int32, shape, len(shape) - 1) < 64


def swap(x):
    return pltpu.roll(x, 64, 1)


def div96(v):
    return (v * 43691) >> 22


def signed(v):
    return jnp.where(v >= L // 2, v - L, v)


def lanes_of(x, index):
    return jnp.take_along_axis(x, index, axis=1, mode="promise_in_bounds")


def slot_facts(m, cols):
    live = m >= 0
    ms = jnp.maximum(m, 0)
    slot = div96(ms)
    z = signed(ms - slot * L)
    col = jnp.where(live, lanes_of(cols, slot), 0)
    xc = div96(col)
    x = signed(xc)
    y = signed(col - xc * L)
    norm = x * x + y * y + z * z
    kin = jnp.where(live, 64.0 * norm.astype(F32) / float(L * L), 0.0)
    zi = z + CUT
    pair = jnp.where(live, zi >> 1, -1)
    lane = jnp.where(live, (zi & 1) * 64 + slot - 64, 0)
    return live, kin, pair, lane


def sticks_kernel(ev, cur, hcur, prev, hprev, gm, scols, wz, res, send, bsend, rt, inv, oh_l, oh_r, y):
    me = lax.axis_index("fft")
    cols = jnp.broadcast_to(scols[pl.ds(me, 1), :], (8, 128))
    row = lax.broadcasted_iota(jnp.int32, (8, 128), 0)
    evc = jnp.zeros((8, 128), F32)
    for b in range(8):
        evc = jnp.where(row == b, ev[b], evc)
    rows32 = lax.broadcasted_iota(jnp.int32, (32, 128), 0)
    rows128 = lax.broadcasted_iota(jnp.int32, (128, 128), 0)
    glo = lax.broadcasted_iota(jnp.int32, (32, 128), 1)
    for k in range(GT):
        at = pl.ds(128 * k, 128)
        d, lo = k // 3, (k % 3) * 128
        live, kin, pair, lane = slot_facts(jnp.broadcast_to(gm[:, at], (8, 128)), cols)
        den = 1.0 + kin
        for c in range(2):
            x, h = cur[c, :, at], hcur[c, :, at]
            r = jnp.where(live, (h - evc * x) / den, 0.0)
            rt[k, 8 * c : 8 * c + 8, :] = r
            res[8 * c : 8 * c + 8, at] = r
            bsend[d, c, :, lo : lo + 128] = jnp.where(live, x, 0.0)
            bsend[d, 2 + c, :, lo : lo + 128] = r
            bsend[d, 4 + c, :, lo : lo + 128] = jnp.where(live, prev[c, :, at], 0.0)
            bsend[d, 6 + c, :, lo : lo + 128] = jnp.where(live, h, 0.0)
            bsend[d, 8 + c, :, lo : lo + 128] = jnp.where(live, hprev[c, :, at], 0.0)
        hit = jnp.broadcast_to(pair[:1], (32, 128)) == rows32
        oh_l[0:32, at] = jnp.where(hit, float(k + 1), 0.0).astype(BF16)
        oh_l[32:64, at] = jnp.where(hit, glo.astype(F32), 0.0).astype(BF16)
        key = jnp.where(live, lane, -1)
        oh_r[:, at] = jnp.where(jnp.broadcast_to(key[:1], (128, 128)) == rows128, 1.0, 0.0).astype(BF16)
    inv[...] = dot_nt(oh_l[...], oh_r[...]).astype(jnp.int32)
    y[400:512, :] = jnp.zeros((112, 128), F32)

    def place(t, carry):
        hi = jnp.broadcast_to(inv[pl.ds(t, 1), :], (16, 128))
        lo = jnp.broadcast_to(inv[pl.ds(t + 32, 1), :], (16, 128))
        acc = jnp.zeros((16, 128), F32)
        for k in range(GT):
            acc = jnp.where(hi == k + 1, lanes_of(rt[k], lo), acc)
        y[pl.ds(pl.multiple_of(t * 16, 16), 16), :] = acc
        return carry

    lax.fori_loop(0, NPAIR, place, 0)
    low = low_lanes((192, 128))
    low96 = low_lanes((96, 128))
    for b2 in range(4):
        parts = []
        for b in (2 * b2, 2 * b2 + 1):
            s = jnp.concatenate([y[pl.ds(c * 8 + b, 32, stride=16), :] for c in range(2)], axis=0)
            hi, lo = halves(s)
            parts.append(jnp.concatenate([hi, lo, hi], axis=0))
        out = dot(wz[...], jnp.concatenate(parts, axis=1))
        for i in range(2):
            o = out[:, 128 * i : 128 * i + 128]
            w = jnp.where(low, o[:192], o[192:])
            w = w + swap(w)
            w = jnp.where(low96, w[:96], w[96:])
            for zl in range(3):
                send[pl.ds((2 * b2 + i) * 3 + zl, 32, stride=24), :] = w[32 * zl : 32 * zl + 32]


def everyone_in(peers_f, peers_b):
    f, b = lax.axis_index("fft"), lax.axis_index("band")
    barrier = pltpu.get_barrier_semaphore()
    if peers_f:
        def greet(i, c):
            pl.semaphore_signal(barrier, inc=1, device_id=(b, lax.rem(f + i, NF)), device_id_type=MESH)
            return c
        lax.fori_loop(1, NF, greet, 0)
    if peers_b:
        def greet_b(i, c):
            pl.semaphore_signal(barrier, inc=1, device_id=(lax.rem(b + i, NBD), f), device_id_type=MESH)
            return c
        lax.fori_loop(1, NBD, greet_b, 0)
    pl.semaphore_wait(barrier, (NF - 1) * peers_f + (NBD - 1) * peers_b)


class FftExchange:
    def __init__(self, src, dst, ssem, rsem, n):
        self.a = (src, dst, ssem, rsem, n)

    def copy(self, to, frm, i):
        src, dst, ssem, rsem, n = self.a
        return pltpu.make_async_remote_copy(
            src_ref=src.at[pl.ds(pl.multiple_of(to * n, 8), n), :],
            dst_ref=dst.at[pl.ds(pl.multiple_of(frm * n, 8), n), :],
            send_sem=ssem.at[i], recv_sem=rsem.at[i],
            device_id=(lax.axis_index("band"), to), device_id_type=MESH)

    def start(self):
        src, dst, ssem, rsem, n = self.a
        f = lax.axis_index("fft")
        def go(i, c):
            self.copy(lax.rem(f + i, NF), f, i).start()
            return c
        lax.fori_loop(1, NF, go, 0)
        own = pl.ds(pl.multiple_of(f * n, 8), n)
        pltpu.make_async_copy(src.at[own, :], dst.at[own, :], rsem.at[0]).start()

    def wait(self):
        src, dst, ssem, rsem, n = self.a
        f = lax.axis_index("fft")
        own = pl.ds(pl.multiple_of(f * n, 8), n)
        pltpu.make_async_copy(src.at[own, :], dst.at[own, :], rsem.at[0]).wait()
        def done(i, c):
            self.copy(lax.rem(f + i, NF), lax.rem(f + NF - i, NF), i).wait()
            return c
        lax.fori_loop(1, NF, done, 0)


class BandExchange:
    def __init__(self, src, dst, place, ssem, rsem):
        self.a = (src, dst, place, ssem, rsem)

    def copy(self, to, frm, i):
        src, dst, place, ssem, rsem = self.a
        return pltpu.make_async_remote_copy(
            src_ref=src.at[to], dst_ref=place(dst, frm), send_sem=ssem.at[i], recv_sem=rsem.at[i],
            device_id=(to, lax.axis_index("fft")), device_id_type=MESH)

    def start(self):
        src, dst, place, ssem, rsem = self.a
        b = lax.axis_index("band")
        for i in range(1, NBD):
            self.copy(lax.rem(b + i, NBD), b, i).start()
        pltpu.make_async_copy(src.at[b], place(dst, b), rsem.at[0]).start()

    def wait(self):
        src, dst, place, ssem, rsem = self.a
        b = lax.axis_index("band")
        pltpu.make_async_copy(src.at[b], place(dst, b), rsem.at[0]).wait()
        for i in range(1, NBD):
            self.copy(lax.rem(b + i, NBD), lax.rem(b + NBD - i, NBD), i).wait()


def band_rows(dst, frm):
    return dst.at[:, pl.ds(pl.multiple_of(frm * 8, 8), 8), :]


def band_slot(dst, frm):
    return dst.at[frm]


def out_kernel(send, bsend, recv, brecv, ssem, rsem, bssem, brsem):
    everyone_in(True, True)
    fx = FftExchange(send, recv, ssem, rsem, 24)
    bx = BandExchange(bsend, brecv, band_rows, bssem, brsem)
    fx.start()
    bx.start()
    fx.wait()
    bx.wait()


def plane_kernel(recv, scols, pot, wy, wxa, wxb, vx, vy, send, q, oh_l, oh_r, inv, pick, pm, tt, potp, gg, gt):
    low1 = low_lanes((1, 128))
    rows32 = lax.broadcasted_iota(jnp.int32, (32, 128), 0)
    rows128 = lax.broadcasted_iota(jnp.int32, (128, 128), 0)
    glo = lax.broadcasted_iota(jnp.int32, (32, 128), 1).astype(F32)
    low = low_lanes((24, 128))
    for k in range(16):
        col = jnp.where(low1, swap(scols[2 * k : 2 * k + 1, :]), scols[2 * k + 1 : 2 * k + 2, :])
        live = col >= 0
        colp = jnp.maximum(col, 0)
        xc = div96(colp)
        xi = signed(xc) + CUT
        yi = signed(colp - xc * L) + CUT
        pair = jnp.where(live, xi >> 1, -1)
        lane = jnp.where(live, (xi & 1) * 64 + yi, -1)
        pick[k : k + 1, :] = pair
        pick[16 + k : 17 + k, :] = jnp.maximum(lane, 0)
        at = pl.ds(128 * k, 128)
        hit = jnp.broadcast_to(pair, (32, 128)) == rows32
        oh_l[0:32, at] = jnp.where(hit, float(k + 1), 0.0).astype(BF16)
        oh_l[32:64, at] = jnp.where(hit, glo, 0.0).astype(BF16)
        oh_r[:, at] = jnp.where(jnp.broadcast_to(lane, (128, 128)) == rows128, 1.0, 0.0).astype(BF16)
        r0, r1 = recv[48 * k : 48 * k + 24, :], recv[48 * k + 24 : 48 * k + 48, :]
        q[k, 0:24, :] = jnp.where(low, r0, swap(r1))
        q[k, 24:48, :] = jnp.where(low, swap(r0), r1)
    inv[...] = dot_nt(oh_l[...], oh_r[...]).astype(jnp.int32)
    potp[...] = jnp.zeros((3, L, 128), F32)
    potp[:, :, 0:L] = pot[...]

    def place(t, carry):
        hi = jnp.broadcast_to(inv[pl.ds(t, 1), :], (48, 128))
        lo = jnp.broadcast_to(inv[pl.ds(t + 32, 1), :], (48, 128))
        acc = jnp.zeros((48, 128), F32)
        for k in range(16):
            acc = jnp.where(hi == k + 1, lanes_of(q[k], lo), acc)
        re, im = acc[:24], acc[24:]
        base = pl.multiple_of(t * 48, 16)
        pm[pl.ds(base, 24), :] = jnp.where(low, re, swap(im))
        pm[pl.ds(base + 24, 24), :] = jnp.where(low, swap(re), im)
        return carry

    lax.fori_loop(0, NPAIR, place, 0)

    def along_y(i, carry):
        at = pl.ds(pl.multiple_of(i * 240, 16), 240)
        hi, lo = halves(pm[at, :])
        out = dot(jnp.concatenate([hi, lo], axis=1), wy[0:256, :]) + dot(hi, wy[256:384, :])
        tt[0, at, :] = out[:, 0:128]
        tt[1, at, :] = out[:, 128:256]
        return carry

    lax.fori_loop(0, 5, along_y, 0)
    tt[:, 1200:1344, :] = jnp.zeros((2, 144, 128), F32)

    def along_x(i, carry):
        his, los = [], []
        for j in range(2):
            s = jnp.concatenate([tt[c, pl.ds(2 * i + j, 56, stride=24), :] for c in range(2)], axis=0)
            hi, lo = halves(s)
            his.append(hi)
            los.append(lo)
        hi = jnp.concatenate(his, axis=1)
        lo = jnp.concatenate(los, axis=1)
        u = dot(wxa[...], jnp.concatenate([hi, lo], axis=0)) + dot(wxb[...], hi)
        pv = jnp.concatenate([potp[lax.rem(2 * i + j, 3)] for j in range(2)], axis=1)
        u = u * jnp.concatenate([pv, pv], axis=0)
        hi, lo = halves(u)
        a = dot(vx[...], hi)
        t = a[0:112] + a[112:224] + dot(vx[0:112, :], lo)
        row = jnp.concatenate(
            [jnp.concatenate([t[0:56, 128 * j : 128 * j + 128], t[56:112, 128 * j : 128 * j + 128]], axis=1) for j in range(2)],
            axis=0)
        hi, lo = halves(row)
        a = dot(hi, vy[...])
        g = a[:, 0:128] + a[:, 128:256] + dot(lo, vy[:, 0:128])
        for j in range(2):
            gg[pl.ds(2 * i + j, 56, stride=24), :] = g[56 * j : 56 * j + 56]
        return carry

    lax.fori_loop(0, 12, along_x, 0)

    def pair_up(t, carry):
        base = pl.multiple_of(t * 48, 16)
        g0, g1 = gg[pl.ds(base, 24), :], gg[pl.ds(base + 24, 24), :]
        gt[t, 0:24, :] = jnp.where(low, g0, swap(g1))
        gt[t, 24:48, :] = jnp.where(low, swap(g0), g1)
        return carry

    lax.fori_loop(0, NPAIR, pair_up, 0)

    def collect(k, carry):
        hi = jnp.broadcast_to(pick[pl.ds(k, 1), :], (48, 128))
        lo = jnp.broadcast_to(pick[pl.ds(k + 16, 1), :], (48, 128))
        acc = jnp.zeros((48, 128), F32)
        for t in range(NPAIR):
            acc = jnp.where(hi == t, lanes_of(gt[t], lo), acc)
        re, im = acc[:24], acc[24:]
        base = pl.multiple_of(k * 48, 16)
        send[pl.ds(base, 24), :] = jnp.where(low, re, swap(im))
        send[pl.ds(base + 24, 24), :] = jnp.where(low, swap(re), im)
        return carry

    lax.fori_loop(0, 16, collect, 0)


def row_side(brecv, qs):
    zero = jnp.zeros((8, 768), F32)
    for d in range(NBD):
        for j in range(3):
            g8 = 3 * d + j
            ty, r0 = g8 // 8, (g8 % 8) * 8
            re, im = brecv[2 * ty, r0 : r0 + 8, :], brecv[2 * ty + 1, r0 : r0 + 8, :]
            o = 64 * d + 8 * j
            qs[o : o + 8, 0:384] = re
            qs[o : o + 8, 384:768] = im
            qs[o + 32 : o + 40, 0:384] = -im
            qs[o + 32 : o + 40, 384:768] = re
        qs[64 * d + 24 : 64 * d + 32, :] = zero
        qs[64 * d + 56 : 64 * d + 64, :] = zero


def back_kernel(send, brecv, recv, early, qs, flat, ks, esend, erecv, ssem, rsem, bssem, brsem):
    everyone_in(True, True)
    fx = FftExchange(send, recv, ssem, rsem, 24)
    fx.start()
    row_side(brecv, qs)
    for m in range(2):
        for ty in range(3):
            at = 64 * ty
            if m == 1 and ty == 1:
                flat[at : at + 64, :] = jnp.zeros((64, 768), F32)
                continue
            src = 2 * ty if m == 0 else (6 if ty == 0 else 8)
            flat[at : at + 64, 0:384] = brecv[src]
            flat[at : at + 64, 384:768] = brecv[src + 1]
        ks[256 * m : 256 * m + 256, :] = jnp.zeros((256, 768), F32)
        for f in range(NF):
            ks[256 * m + 8 * f : 256 * m + 8 * f + 6, :] = flat[6 * f : 6 * f + 6, :]
    khi, klo = halves(ks[...])
    low = low_lanes((256, 128))
    for n in range(2):
        qhi, qlo = halves(qs[256 * n : 256 * n + 256, :])
        g = dot_nt(khi, qhi) + dot_nt(klo, qhi) + dot_nt(khi, qlo)
        for j in range(2):
            c, h = g[0:256, 128 * j : 128 * j + 128], g[256:512, 128 * j : 128 * j + 128]
            esend[4 * n + 2 * j] = jnp.where(low, c, swap(h))
            esend[4 * n + 2 * j + 1] = jnp.where(low, swap(c), h)
    bx = BandExchange(esend, erecv, band_slot, bssem, brsem)
    bx.start()
    bx.wait()
    total = erecv[0]
    for d in range(1, NBD):
        total = total + erecv[d]
    early[...] = total
    fx.wait()


def term_kernel(recv, res, gm, scols, vza, vzb, hres, hsend, z, zt):
    for b2 in range(4):
        his, los = [], []
        for b in (2 * b2, 2 * b2 + 1):
            s = jnp.concatenate([recv[pl.ds(3 * b + zl, 32, stride=24), :] for zl in range(3)], axis=0)
            hi, lo = halves(s)
            his.append(hi)
            los.append(lo)
        hi = jnp.concatenate(his, axis=1)
        lo = jnp.concatenate(los, axis=1)
        out = dot(vza[...], jnp.concatenate([hi, lo], axis=0)) + dot(vzb[...], hi)
        low = low_lanes((64, 128))
        for i in range(2):
            o = out[:, 128 * i : 128 * i + 128]
            other = swap(o[64:128])
            z[pl.ds(2 * b2 + i, 64, stride=8), :] = o[0:64] + jnp.where(low, other, -other)
    low = low_lanes((8, 128))
    for t in range(NPAIR):
        z0, z1 = z[16 * t : 16 * t + 8, :], z[16 * t + 8 : 16 * t + 16, :]
        zt[t, 0:8, :] = jnp.where(low, z0, swap(z1))
        zt[t, 8:16, :] = jnp.where(low, swap(z0), z1)
    me = lax.axis_index("fft")
    cols = jnp.broadcast_to(scols[pl.ds(me, 1), :], (8, 128))
    for k in range(GT):
        at = pl.ds(128 * k, 128)
        live, kin, pair, lane = slot_facts(jnp.broadcast_to(gm[:, at], (8, 128)), cols)
        hi = jnp.concatenate([pair, pair], axis=0)
        lo = jnp.concatenate([lane, lane], axis=0)
        acc = jnp.zeros((16, 128), F32)
        for t in range(NPAIR):
            acc = jnp.where(hi == t, lanes_of(zt[t], lo), acc)
        for c in range(2):
            v = kin * res[8 * c : 8 * c + 8, at] + acc[8 * c : 8 * c + 8] * (1.0 / float(L**3))
            v = jnp.where(live, v, 0.0)
            hres[c, :, at] = v
            hsend[k // 3, c, :, (k % 3) * 128 : (k % 3) * 128 + 128] = v


F0, F1 = 10, 22


def late_kernel(hsend, brecv, early, out, hrecv, qs, flat, ks, lsend, lrecv, fsend, frecv,
                hssem, hrsem, bssem, brsem, ssem, rsem):
    everyone_in(True, True)
    hx = BandExchange(hsend, hrecv, band_rows, hssem, hrsem)
    hx.start()
    row_side(brecv, qs)
    ks[...] = jnp.zeros((96, 768), F32)
    hx.wait()
    flat[:, 0:384] = hrecv[0]
    flat[:, 384:768] = hrecv[1]
    for f in range(F0, F1):
        k0, k1 = max(6 * f, 64), min(6 * f + 6, 128)
        o = 8 * (f - F0) + k0 - 6 * f
        ks[o : o + k1 - k0, :] = flat[k0 - 64 : k1 - 64, :]
    khi, klo = halves(ks[...])
    low = low_lanes((48, 128))
    for n in range(2):
        qhi, qlo = halves(qs[256 * n : 256 * n + 256, :])
        g = dot_nt(khi, qhi) + dot_nt(klo, qhi) + dot_nt(khi, qlo)
        for j in range(2):
            a, b = g[0:48, 128 * j : 128 * j + 128], g[48:96, 128 * j : 128 * j + 128]
            lsend[4 * n + 2 * j] = jnp.where(low, a, swap(b))
            lsend[4 * n + 2 * j + 1] = jnp.where(low, swap(a), b)
    bx = BandExchange(lsend, lrecv, band_slot, bssem, brsem)
    bx.start()
    fsend[...] = early[...]
    bx.wait()
    total = lrecv[0]
    for d in range(1, NBD):
        total = total + lrecv[d]
    fsend[8 * F0 : 8 * F0 + 48, :] = fsend[8 * F0 : 8 * F0 + 48, :] + jnp.where(low, 0.0, swap(total))
    fsend[8 * F0 + 48 : 8 * F0 + 96, :] = fsend[8 * F0 + 48 : 8 * F0 + 96, :] + jnp.where(low, 0.0, total)
    fx = FftExchange(fsend, frecv, ssem, rsem, 8)
    fx.start()
    fx.wait()
    total = frecv[0:8, :]
    for d in range(1, NF):
        total = total + frecv[8 * d : 8 * d + 8, :]
    out[...] = total * (8.0 / float(L**3))


def sds(*shape):
    return jax.ShapeDtypeStruct(shape, F32)


DMA = pltpu.SemaphoreType.DMA
BIG = 48 * 1024 * 1024


def local(current, h_current, previous, h_previous, eigen_values, potential, stick_cols, g_map):
    w = tables()
    gm = g_map.reshape(1, 3072)
    sc = stick_cols.reshape(NF, 128)
    params = functools.partial(pltpu.CompilerParams, vmem_limit_bytes=BIG)
    res, send, bsend = pl.pallas_call(
        sticks_kernel,
        out_shape=(sds(16, 3072), sds(768, 128), sds(8, 10, 8, 384)),
        in_specs=[SM] + [VM] * 7, out_specs=(VM, VM, VM),
        scratch_shapes=[
            pltpu.VMEM((24, 16, 128), F32), pltpu.VMEM((64, 128), jnp.int32),
            pltpu.VMEM((64, 3072), BF16), pltpu.VMEM((128, 3072), BF16), pltpu.VMEM((512, 128), F32)],
        compiler_params=params(), name="sticks",
    )(eigen_values, current, h_current, previous, h_previous, gm, sc, w["wz"])
    recv, brecv = pl.pallas_call(
        out_kernel, out_shape=(sds(768, 128), sds(10, 64, 384)), in_specs=[VM, VM], out_specs=(VM, VM),
        scratch_shapes=[DMA((NF,)), DMA((NF,)), DMA((NBD,)), DMA((NBD,))],
        compiler_params=params(collective_id=0, has_side_effects=True), name="outward",
    )(send, bsend)
    send2 = pl.pallas_call(
        plane_kernel, out_shape=sds(768, 128), in_specs=[VM] * 8, out_specs=VM,
        scratch_shapes=[
            pltpu.VMEM((16, 48, 128), F32), pltpu.VMEM((64, 2048), BF16), pltpu.VMEM((128, 2048), BF16),
            pltpu.VMEM((64, 128), jnp.int32), pltpu.VMEM((32, 128), jnp.int32), pltpu.VMEM((1200, 128), F32),
            pltpu.VMEM((2, 1344, 128), F32), pltpu.VMEM((3, L, 128), F32), pltpu.VMEM((1344, 128), F32),
            pltpu.VMEM((NPAIR, 48, 128), F32)],
        compiler_params=params(), name="planes",
    )(recv, sc, potential, w["wy"], w["wxa"], w["wxb"], w["vx"], w["vy"])
    recv2, early = pl.pallas_call(
        back_kernel, out_shape=(sds(768, 128), sds(256, 128)), in_specs=[VM, VM], out_specs=(VM, VM),
        scratch_shapes=[
            pltpu.VMEM((512, 768), F32), pltpu.VMEM((192, 768), F32), pltpu.VMEM((512, 768), F32),
            pltpu.VMEM((8, 256, 128), F32), pltpu.VMEM((8, 256, 128), F32),
            DMA((NF,)), DMA((NF,)), DMA((NBD,)), DMA((NBD,))],
        compiler_params=params(collective_id=1, has_side_effects=True), name="inward",
    )(send2, brecv)
    hres, hsend = pl.pallas_call(
        term_kernel, out_shape=(sds(2, 8, 3072), sds(8, 2, 8, 384)), in_specs=[VM] * 6, out_specs=(VM, VM),
        scratch_shapes=[pltpu.VMEM((512, 128), F32), pltpu.VMEM((NPAIR, 16, 128), F32)],
        compiler_params=params(), name="term",
    )(recv2, res, gm, sc, w["vza"], w["vzb"])
    tile = pl.pallas_call(
        late_kernel, out_shape=sds(8, 128), in_specs=[VM] * 3, out_specs=VM,
        scratch_shapes=[
            pltpu.VMEM((2, 64, 384), F32), pltpu.VMEM((512, 768), F32), pltpu.VMEM((64, 768), F32),
            pltpu.VMEM((96, 768), F32), pltpu.VMEM((8, 48, 128), F32), pltpu.VMEM((8, 48, 128), F32),
            pltpu.VMEM((256, 128), F32), pltpu.VMEM((256, 128), F32),
            DMA((NBD,)), DMA((NBD,)), DMA((NBD,)), DMA((NBD,)), DMA((NF,)), DMA((NF,))],
        compiler_params=params(collective_id=2, has_side_effects=True), name="late",
    )(hsend, brecv, early)
    mats = jnp.transpose(tile[0:6].reshape(6, 4, 32)[:, :, 0:24], (1, 2, 0))
    return hres, mats[0:2], mats[2:4]


def solution(mesh):
    bf = P(None, "band", "fft")
    in_specs = (bf, bf, bf, bf, P("band"), P("fft", None, None), P(), P("fft"))
    return jax.shard_map(local, mesh=mesh, in_specs=in_specs, out_specs=(bf, bf, bf), check_vma=False)
```

time: 777 us -> 103 us (0.13); the launches traced: 768 us -> 102 us
  local copies, waits for them, and re-layouts: 404 us -> 7.46 us
  waiting for transfers between devices: 256 us -> 0 us
  Pallas kernels: 0 us -> 93.7 us
  blocking collectives: 27.7 us -> 0 us
  other arithmetic: 22.8 us -> 0 us
  matrix products: 21.2 us -> 0 us
  starting transfers between devices: 21.1 us -> 0 us
  between operations: 15.1 us -> 0.83 us
    psum x1 -> x0, waiting for transfers between devices: 253 us -> none  [local(): summed = lax.psum(partial_value, ('band', 'fft'))]
    gather x10 -> x0, local copies, waits for them, and re-layouts: 163 us -> none  [the longest x2 94.1 us: local(): jnp.take(residual_rows, slot_inverse, axis=0)]
    unnamed x27 -> x36, local copies, waits for them, and re-layouts: 114 us -> 6.77 us
    pallas_call x0 -> x6, Pallas kernels: none -> 93.7 us  [the longest x1 22.6 us: local(): pl.pallas_call(late_kernel, out_shape=sds(8, 128), in_specs=[VM] * 3, out...]
    all_to_all x6 -> x0, local copies, waits for them, and re-layouts: 31.3 us -> none  [the longest x2 14.8 us: local(): lax.all_to_all(picked, 'fft', split_axis=3, concat_axis=2, tiled=True)]
    all_to_all x1 -> x0, blocking collectives: 27.7 us -> none  [local(): lax.all_to_all(picked, 'fft', split_axis=3, concat_axis=2, tiled=True)]
    scatter x2 -> x0, local copies, waits for them, and re-layouts: 27.3 us -> none  [the longest x1 15.5 us: local(): plane_inverse = jnp.full((plane_count,), stick_total, jnp.int32).at[place...]
    transpose x6 -> x1, local copies, waits for them, and re-layouts: 21.5 us -> 0.01 us  [local(): mats = jnp.transpose(tile[0:6].reshape(6, 4, 32)[:, :, 0:24], (1, 2, 0))]
  transfers between devices with their start and end apart: 4 -> 0, of which waited for: 2 -> 0; matrix products, arithmetic and copies ran while one was open for 10% -> 0% of each run, Pallas kernels for 0% -> 0%
where the time goes in v1:
time: 103 us; the launch traced here: 102 us
  Pallas kernels  93.7 us (91%)
  local copies, waits for them, and re-layouts  7.46 us (7%)
    pallas_call x1, Pallas kernels, local(): pl.pallas_call(late_kernel, out_shape=sds(8, 128), in_specs=[VM] * 3, out...  22.6 us
    pallas_call x1, Pallas kernels, local(): pl.pallas_call(out_kernel, out_shape=(sds(768, 128), sds(10, 64, 384)), i...  21.8 us
    pallas_call x1, Pallas kernels, local(): pl.pallas_call(plane_kernel, out_shape=sds(768, 128), in_specs=[VM] * 8,...  21.5 us
    pallas_call x1, Pallas kernels, local(): pl.pallas_call(back_kernel, out_shape=(sds(768, 128), sds(256, 128)), in_...  20.2 us
    unnamed x36, local copies, waits for them, and re-layouts  6.77 us
    pallas_call x1, Pallas kernels, local(): pl.pallas_call(sticks_kernel, out_shape=(sds(16, 3072), sds(768, 128), sd...  4.94 us
    pallas_call x1, Pallas kernels, local(): pl.pallas_call(term_kernel, out_shape=(sds(2, 8, 3072), sds(8, 2, 8, 384)...  2.66 us

profile of v1, /device:TPU:4, one launch (start us, length us, event | category | flops | bytes accessed | tf_op | source)
XLA Modules:
  0.0 102.0 jit_solution(17781775207152480790)
XLA Ops:
  0.6 0.6 copy-done.17
  1.3 0.9 copy-done
  2.2 0.9 copy-done.1
  3.1 0.9 copy-done.2
  4.1 0.9 copy-done.3
  5.0 0.9 copy-done.4
  5.9 0.7 copy-done.6
  6.6 0.7 copy-done.14
  7.3 4.9 %sticks.1 = (f32[16,3072]{1,0:T(8,128)S(1)}, f32[768,128]{1,0:T(8,128)S(1)}, f32[8,10,8,384]{3,2,1,0:T(8,128)S(1)}) custom-call(f32[8]{0:T(128)S(1)} %copy-done.17, f32[2,8,3072]{2,1,0:T(8,128)S(1)} %copy-done, f32[2,8,3072]{2,1,0:T(8,128)S(1)} %copy-done.1, f32[2,8,3072]{2,1,0:T(8,128)S(1)} %copy-done.2, f32[2,8,3072]{2,1,0:T(8,128)S(1)} %copy-done.3, ...), custom_call_target="tpu_custom_call" | custom-call | tf_op jit(solution)/shard_map/sticks/pallas_call | solution.py:532
  12.3 0.0 copy-start.5
  12.3 0.0 copy-start.7
  12.3 0.0 copy-start.8
  12.3 0.0 copy-start.9
  12.3 0.0 copy-start.10
  12.4 0.0 copy-start.11
  12.4 0.0 copy-start.13
  12.4 21.8 %outward.1 = (f32[768,128]{1,0:T(8,128)S(1)}, f32[10,64,384]{2,1,0:T(8,128)S(1)}) custom-call(f32[768,128]{1,0:T(8,128)S(1)} %get-tuple-element.12.send, f32[8,10,8,384]{3,2,1,0:T(8,128)S(1)} %get-tuple-element.13.bsend), custom_call_target="tpu_custom_call" | custom-call | tf_op jit(solution)/shard_map/outward/pallas_call | solution.py:541
  34.3 21.5 %planes.1.send = f32[768,128]{1,0:T(8,128)S(1)} custom-call(f32[768,128]{1,0:T(8,128)S(1)} %get-tuple-element.14.recv, s32[32,128]{1,0:T(8,128)S(1)} %bitcast.6, f32[3,96,96]{2,1,0:T(8,128)S(1)} %copy-done.8, bf16[384,256]{1,0:T(8,128)(2,1)S(1)} %copy-done.5, bf16[192,224]{1,0:T(8,128)(2,1)S(1)} %copy-done.11, bf16[192,112]{1,0:T(8,128)(2,1)S(1)} %copy-done.13, ...), custom_call_target="tpu_custom_call" | custom-call | tf_op jit(solution)/shard_map/planes/pallas_call | solution.py:546
  55.8 0.0 copy-start.16
  55.9 20.2 %inward.1 = (f32[768,128]{1,0:T(8,128)S(1)}, f32[256,128]{1,0:T(8,128)S(1)}) custom-call(f32[768,128]{1,0:T(8,128)S(1)} %planes.1.send, f32[10,64,384]{2,1,0:T(8,128)S(1)} %get-tuple-element.15.brecv), custom_call_target="tpu_custom_call" | custom-call | tf_op jit(solution)/shard_map/inward/pallas_call | solution.py:555
  76.1 2.7 %term.1 = (f32[2,8,3072]{2,1,0:T(8,128)}, f32[8,2,8,384]{3,2,1,0:T(8,128)S(1)}) custom-call(f32[768,128]{1,0:T(8,128)S(1)} %get-tuple-element.16.recv, f32[16,3072]{1,0:T(8,128)S(1)} %get-tuple-element.17.res, s32[1,3072]{1,0:T(1,128)S(1)} %bitcast.9, s32[32,128]{1,0:T(8,128)S(1)} %bitcast.7, bf16[128,192]{1,0:T(8,128)(2,1)S(1)} %copy-done.12, ...), custom_call_target="tpu_custom_call" | custom-call | tf_op jit(solution)/shard_map/term/pallas_call | solution.py:563
  78.8 22.6 %late.1 = f32[8,128]{1,0:T(8,128)S(1)} custom-call(f32[8,2,8,384]{3,2,1,0:T(8,128)S(1)} %get-tuple-element.19.hsend, f32[10,64,384]{2,1,0:T(8,128)S(1)} %get-tuple-element.15.brecv, f32[256,128]{1,0:T(8,128)S(1)} %get-tuple-element.20.early), custom_call_target="tpu_custom_call" | custom-call | tf_op jit(solution)/shard_map/late/pallas_call | solution.py:568
  101.3 0.1 reshape.17
  101.4 0.6 fusion
  (21 shorter events, 0.0 us)
Async XLA Ops:
  0.6 0.7 copy-start.17
  1.3 0.9 copy-start
  2.2 0.9 copy-start.1
  3.1 0.9 copy-start.2
  4.1 0.9 copy-start.3
  5.0 0.9 copy-start.4
  5.9 0.7 copy-start.6
  6.6 0.7 copy-start.14
  12.3 21.9 %copy-start.5 = (bf16[384,256]{1,0:T(8,128)(2,1)S(1)}, bf16[384,256]{1,0:T(8,128)(2,1)}, u32[]{:S(2)}) copy-start(bf16[384,256]{1,0:T(8,128)(2,1)} %constant.17.clone.wy) | copy-start | bytes 589828
  12.3 21.9 %copy-start.7 = (s32[4096]{0:T(1024)S(1)}, s32[4096]{0:T(1024)}, u32[]{:S(2)}) copy-start(s32[4096]{0:T(1024)} %param.22) | copy-start | bytes 49156
  12.3 21.9 %copy-start.8 = (f32[3,96,96]{2,1,0:T(8,128)S(1)}, f32[3,96,96]{2,1,0:T(8,128)}, u32[]{:S(2)}) copy-start(f32[3,96,96]{2,1,0:T(8,128)} %pot.1) | copy-start | bytes 331780
  12.3 21.9 %copy-start.9 = (bf16[256,256]{1,0:T(8,128)(2,1)S(1)}, bf16[256,256]{1,0:T(8,128)(2,1)}, u32[]{:S(2)}) copy-start(bf16[256,256]{1,0:T(8,128)(2,1)} %constant.21.clone.vy) | copy-start | bytes 393220
  12.3 21.9 %copy-start.10 = (bf16[224,192]{1,0:T(8,128)(2,1)S(1)}, bf16[224,192]{1,0:T(8,128)(2,1)}, u32[]{:S(2)}) copy-start(bf16[224,192]{1,0:T(8,128)(2,1)} %constant.20.clone.vx) | copy-start | bytes 258052
  12.4 21.9 %copy-start.11 = (bf16[192,224]{1,0:T(8,128)(2,1)S(1)}, bf16[192,224]{1,0:T(8,128)(2,1)}, u32[]{:S(2)}) copy-start(bf16[192,224]{1,0:T(8,128)(2,1)} %constant.18.clone.wxa) | copy-start | bytes 258052
  12.4 21.9 %copy-start.13 = (bf16[192,112]{1,0:T(8,128)(2,1)S(1)}, bf16[192,112]{1,0:T(8,128)(2,1)}, u32[]{:S(2)}) copy-start(bf16[192,112]{1,0:T(8,128)(2,1)} %constant.19.clone.wxb) | copy-start | bytes 129028
  55.8 20.2 %copy-start.12 = (bf16[128,192]{1,0:T(8,128)(2,1)S(1)}, bf16[128,192]{1,0:T(8,128)(2,1)}, u32[]{:S(2)}) copy-start(bf16[128,192]{1,0:T(8,128)(2,1)} %constant.22.clone.vza) | copy-start | bytes 147460
  55.8 20.2 %copy-start.15 = (s32[3072]{0:T(1024)S(1)}, s32[3072]{0:T(1024)}, u32[]{:S(2)}) copy-start(s32[3072]{0:T(1024)} %param.23) | copy-start | bytes 36868
  55.8 20.2 %copy-start.16 = (bf16[128,96]{1,0:T(8,128)(2,1)S(1)}, bf16[128,96]{1,0:T(8,128)(2,1)}, u32[]{:S(2)}) copy-start(bf16[128,96]{1,0:T(8,128)(2,1)} %constant.23.clone.vzb) | copy-start | bytes 73732

commit v2 on v1

--- a/solution.py
+++ b/solution.py
@@ -1,4 +1,3 @@
-import functools
 import math
 
 import jax
@@ -20,6 +19,7 @@
 NPAIR = 25
 MESH = pl.DeviceIdType.MESH
 VM = pl.BlockSpec(memory_space=pltpu.VMEM)
+HB = pl.BlockSpec(memory_space=pltpu.HBM)
 SM = pl.BlockSpec(memory_space=pltpu.SMEM)
 
 
@@ -185,20 +185,24 @@
                 send[pl.ds((2 * b2 + i) * 3 + zl, 32, stride=24), :] = w[32 * zl : 32 * zl + 32]
 
 
-def everyone_in(peers_f, peers_b):
+def greet_everyone():
     f, b = lax.axis_index("fft"), lax.axis_index("band")
     barrier = pltpu.get_barrier_semaphore()
-    if peers_f:
-        def greet(i, c):
-            pl.semaphore_signal(barrier, inc=1, device_id=(b, lax.rem(f + i, NF)), device_id_type=MESH)
-            return c
-        lax.fori_loop(1, NF, greet, 0)
-    if peers_b:
-        def greet_b(i, c):
-            pl.semaphore_signal(barrier, inc=1, device_id=(lax.rem(b + i, NBD), f), device_id_type=MESH)
-            return c
-        lax.fori_loop(1, NBD, greet_b, 0)
-    pl.semaphore_wait(barrier, (NF - 1) * peers_f + (NBD - 1) * peers_b)
+
+    def greet(i, c):
+        pl.semaphore_signal(barrier, inc=1, device_id=(b, lax.rem(f + i, NF)), device_id_type=MESH)
+        return c
+
+    def greet_b(i, c):
+        pl.semaphore_signal(barrier, inc=1, device_id=(lax.rem(b + i, NBD), f), device_id_type=MESH)
+        return c
+
+    lax.fori_loop(1, NF, greet, 0)
+    lax.fori_loop(1, NBD, greet_b, 0)
+
+
+def everyone_in():
+    pl.semaphore_wait(pltpu.get_barrier_semaphore(), NF - 1 + NBD - 1)
 
 
 class FftExchange:
@@ -267,22 +271,11 @@
     return dst.at[frm]
 
 
-def out_kernel(send, bsend, recv, brecv, ssem, rsem, bssem, brsem):
-    everyone_in(True, True)
-    fx = FftExchange(send, recv, ssem, rsem, 24)
-    bx = BandExchange(bsend, brecv, band_rows, bssem, brsem)
-    fx.start()
-    bx.start()
-    fx.wait()
-    bx.wait()
-
-
-def plane_kernel(recv, scols, pot, wy, wxa, wxb, vx, vy, send, q, oh_l, oh_r, inv, pick, pm, tt, potp, gg, gt):
+def plane_maps(scols, pot, oh_l, oh_r, inv, pick, potp):
     low1 = low_lanes((1, 128))
     rows32 = lax.broadcasted_iota(jnp.int32, (32, 128), 0)
     rows128 = lax.broadcasted_iota(jnp.int32, (128, 128), 0)
     glo = lax.broadcasted_iota(jnp.int32, (32, 128), 1).astype(F32)
-    low = low_lanes((24, 128))
     for k in range(16):
         col = jnp.where(low1, swap(scols[2 * k : 2 * k + 1, :]), scols[2 * k + 1 : 2 * k + 2, :])
         live = col >= 0
@@ -299,12 +292,17 @@
         oh_l[0:32, at] = jnp.where(hit, float(k + 1), 0.0).astype(BF16)
         oh_l[32:64, at] = jnp.where(hit, glo, 0.0).astype(BF16)
         oh_r[:, at] = jnp.where(jnp.broadcast_to(lane, (128, 128)) == rows128, 1.0, 0.0).astype(BF16)
+    inv[...] = dot_nt(oh_l[...], oh_r[...]).astype(jnp.int32)
+    potp[...] = jnp.zeros((3, L, 128), F32)
+    potp[:, :, 0:L] = pot[...]
+
+
+def planes(recv, wy, wxa, wxb, vx, vy, send, q, inv, pick, pm, tt, potp, gg, gt):
+    low = low_lanes((24, 128))
+    for k in range(16):
         r0, r1 = recv[48 * k : 48 * k + 24, :], recv[48 * k + 24 : 48 * k + 48, :]
         q[k, 0:24, :] = jnp.where(low, r0, swap(r1))
         q[k, 24:48, :] = jnp.where(low, swap(r0), r1)
-    inv[...] = dot_nt(oh_l[...], oh_r[...]).astype(jnp.int32)
-    potp[...] = jnp.zeros((3, L, 128), F32)
-    potp[:, :, 0:L] = pot[...]
 
     def place(t, carry):
         hi = jnp.broadcast_to(inv[pl.ds(t, 1), :], (48, 128))
@@ -398,11 +396,7 @@
         qs[64 * d + 56 : 64 * d + 64, :] = zero
 
 
-def back_kernel(send, brecv, recv, early, qs, flat, ks, esend, erecv, ssem, rsem, bssem, brsem):
-    everyone_in(True, True)
-    fx = FftExchange(send, recv, ssem, rsem, 24)
-    fx.start()
-    row_side(brecv, qs)
+def early_gram(brecv, qs, flat, ks, esend):
     for m in range(2):
         for ty in range(3):
             at = 64 * ty
@@ -424,15 +418,6 @@
             c, h = g[0:256, 128 * j : 128 * j + 128], g[256:512, 128 * j : 128 * j + 128]
             esend[4 * n + 2 * j] = jnp.where(low, c, swap(h))
             esend[4 * n + 2 * j + 1] = jnp.where(low, swap(c), h)
-    bx = BandExchange(esend, erecv, band_slot, bssem, brsem)
-    bx.start()
-    bx.wait()
-    total = erecv[0]
-    for d in range(1, NBD):
-        total = total + erecv[d]
-    early[...] = total
-    fx.wait()
-
 
 def term_kernel(recv, res, gm, scols, vza, vzb, hres, hsend, z, zt):
     for b2 in range(4):
@@ -475,16 +460,10 @@
 F0, F1 = 10, 22
 
 
-def late_kernel(hsend, brecv, early, out, hrecv, qs, flat, ks, lsend, lrecv, fsend, frecv,
-                hssem, hrsem, bssem, brsem, ssem, rsem):
-    everyone_in(True, True)
-    hx = BandExchange(hsend, hrecv, band_rows, hssem, hrsem)
-    hx.start()
-    row_side(brecv, qs)
+def late_gram(hrecv, qs, flat, ks, lsend):
     ks[...] = jnp.zeros((96, 768), F32)
-    hx.wait()
-    flat[:, 0:384] = hrecv[0]
-    flat[:, 384:768] = hrecv[1]
+    flat[0:64, 0:384] = hrecv[0]
+    flat[0:64, 384:768] = hrecv[1]
     for f in range(F0, F1):
         k0, k1 = max(6 * f, 64), min(6 * f + 6, 128)
         o = 8 * (f - F0) + k0 - 6 * f
@@ -498,22 +477,71 @@
             a, b = g[0:48, 128 * j : 128 * j + 128], g[48:96, 128 * j : 128 * j + 128]
             lsend[4 * n + 2 * j] = jnp.where(low, a, swap(b))
             lsend[4 * n + 2 * j + 1] = jnp.where(low, swap(a), b)
-    bx = BandExchange(lsend, lrecv, band_slot, bssem, brsem)
-    bx.start()
-    fsend[...] = early[...]
-    bx.wait()
+
+
+def step_kernel(ev, cur_h, hcur_h, prev_h, hprev_h, gm_h, scols_h, pot_h, wz_h, wy_h, wxa_h, wxb_h, vx_h, vy_h,
+                vza_h, vzb_h, hres_h, out,
+                cur, hcur, prev, hprev, gm, scols, pot, wz, wy, wxa, wxb, vx, vy, vza, vzb, hres,
+                res, send, bsend, rt, zinv, zoh_l, zoh_r, y,
+                recv, brecv, oh_l, oh_r, inv, pick, potp, q, pm, tt, gg, gt, send2, recv2,
+                qs, flat, ks, esend, erecv, z, zt, hsend, hrecv, lks, lsend, lrecv, fsend, frecv,
+                s1, r1, s2, r2, s3, r3, s4, r4, s5, r5, s6, r6, s7, r7, load):
+    pairs = [(gm_h, gm), (scols_h, scols), (cur_h, cur), (hcur_h, hcur), (prev_h, prev), (hprev_h, hprev), (wz_h, wz),
+             (pot_h, pot), (wy_h, wy), (wxa_h, wxa), (wxb_h, wxb), (vx_h, vx), (vy_h, vy), (vza_h, vza), (vzb_h, vzb)]
+    loads = [pltpu.make_async_copy(a, b, load.at[i]) for i, (a, b) in enumerate(pairs)]
+    for copy in loads:
+        copy.start()
+    greet_everyone()
+    for copy in loads[:7]:
+        copy.wait()
+    sticks_kernel(ev, cur, hcur, prev, hprev, gm, scols, wz, res, send, bsend, rt, zinv, zoh_l, zoh_r, y)
+    everyone_in()
+    x1 = FftExchange(send, recv, s1, r1, 24)
+    x2 = BandExchange(bsend, brecv, band_rows, s2, r2)
+    x3 = FftExchange(send2, recv2, s3, r3, 24)
+    x4 = BandExchange(esend, erecv, band_slot, s4, r4)
+    x5 = BandExchange(hsend, hrecv, band_rows, s5, r5)
+    x6 = BandExchange(lsend, lrecv, band_slot, s6, r6)
+    x7 = FftExchange(fsend, frecv, s7, r7, 8)
+    x1.start()
+    x2.start()
+    for copy in loads[7:]:
+        copy.wait()
+    plane_maps(scols, pot, oh_l, oh_r, inv, pick, potp)
+    x1.wait()
+    planes(recv, wy, wxa, wxb, vx, vy, send2, q, inv, pick, pm, tt, potp, gg, gt)
+    x3.start()
+    x2.wait()
+    row_side(brecv, qs)
+    early_gram(brecv, qs, flat, ks, esend)
+    x4.start()
+    x3.wait()
+    term_kernel(recv2, res, gm, scols, vza, vzb, hres, hsend, z, zt)
+    x5.start()
+    store = pltpu.make_async_copy(hres, hres_h, load.at[15])
+    store.start()
+    x4.wait()
+    total = erecv[0]
+    for d in range(1, NBD):
+        total = total + erecv[d]
+    fsend[...] = total
+    x5.wait()
+    late_gram(hrecv, qs, flat, lks, lsend)
+    x6.start()
+    x6.wait()
+    low = low_lanes((48, 128))
     total = lrecv[0]
     for d in range(1, NBD):
         total = total + lrecv[d]
     fsend[8 * F0 : 8 * F0 + 48, :] = fsend[8 * F0 : 8 * F0 + 48, :] + jnp.where(low, 0.0, swap(total))
     fsend[8 * F0 + 48 : 8 * F0 + 96, :] = fsend[8 * F0 + 48 : 8 * F0 + 96, :] + jnp.where(low, 0.0, total)
-    fx = FftExchange(fsend, frecv, ssem, rsem, 8)
-    fx.start()
-    fx.wait()
+    x7.start()
+    x7.wait()
     total = frecv[0:8, :]
     for d in range(1, NF):
         total = total + frecv[8 * d : 8 * d + 8, :]
     out[...] = total * (8.0 / float(L**3))
+    store.wait()
 
 
 def sds(*shape):
@@ -521,59 +549,36 @@
 
 
 DMA = pltpu.SemaphoreType.DMA
-BIG = 48 * 1024 * 1024
+BIG = 64 * 1024 * 1024
 
 
 def local(current, h_current, previous, h_previous, eigen_values, potential, stick_cols, g_map):
     w = tables()
     gm = g_map.reshape(1, 3072)
     sc = stick_cols.reshape(NF, 128)
-    params = functools.partial(pltpu.CompilerParams, vmem_limit_bytes=BIG)
-    res, send, bsend = pl.pallas_call(
-        sticks_kernel,
-        out_shape=(sds(16, 3072), sds(768, 128), sds(8, 10, 8, 384)),
-        in_specs=[SM] + [VM] * 7, out_specs=(VM, VM, VM),
+    vm = lambda *shape: pltpu.VMEM(shape, F32)
+    v16 = lambda *shape: pltpu.VMEM(shape, BF16)
+    vi = lambda *shape: pltpu.VMEM(shape, jnp.int32)
+    sems = []
+    for n in (NF, NBD, NF, NBD, NBD, NBD, NF):
+        sems += [DMA((n,)), DMA((n,))]
+    hres, tile = pl.pallas_call(
+        step_kernel, out_shape=(sds(2, 8, 3072), sds(8, 128)), in_specs=[SM] + [HB] * 15, out_specs=(HB, VM),
         scratch_shapes=[
-            pltpu.VMEM((24, 16, 128), F32), pltpu.VMEM((64, 128), jnp.int32),
-            pltpu.VMEM((64, 3072), BF16), pltpu.VMEM((128, 3072), BF16), pltpu.VMEM((512, 128), F32)],
-        compiler_params=params(), name="sticks",
-    )(eigen_values, current, h_current, previous, h_previous, gm, sc, w["wz"])
-    recv, brecv = pl.pallas_call(
-        out_kernel, out_shape=(sds(768, 128), sds(10, 64, 384)), in_specs=[VM, VM], out_specs=(VM, VM),
-        scratch_shapes=[DMA((NF,)), DMA((NF,)), DMA((NBD,)), DMA((NBD,))],
-        compiler_params=params(collective_id=0, has_side_effects=True), name="outward",
-    )(send, bsend)
-    send2 = pl.pallas_call(
-        plane_kernel, out_shape=sds(768, 128), in_specs=[VM] * 8, out_specs=VM,
-        scratch_shapes=[
-            pltpu.VMEM((16, 48, 128), F32), pltpu.VMEM((64, 2048), BF16), pltpu.VMEM((128, 2048), BF16),
-            pltpu.VMEM((64, 128), jnp.int32), pltpu.VMEM((32, 128), jnp.int32), pltpu.VMEM((1200, 128), F32),
-            pltpu.VMEM((2, 1344, 128), F32), pltpu.VMEM((3, L, 128), F32), pltpu.VMEM((1344, 128), F32),
-            pltpu.VMEM((NPAIR, 48, 128), F32)],
-        compiler_params=params(), name="planes",
-    )(recv, sc, potential, w["wy"], w["wxa"], w["wxb"], w["vx"], w["vy"])
-    recv2, early = pl.pallas_call(
-        back_kernel, out_shape=(sds(768, 128), sds(256, 128)), in_specs=[VM, VM], out_specs=(VM, VM),
-        scratch_shapes=[
-            pltpu.VMEM((512, 768), F32), pltpu.VMEM((192, 768), F32), pltpu.VMEM((512, 768), F32),
-            pltpu.VMEM((8, 256, 128), F32), pltpu.VMEM((8, 256, 128), F32),
-            DMA((NF,)), DMA((NF,)), DMA((NBD,)), DMA((NBD,))],
-        compiler_params=params(collective_id=1, has_side_effects=True), name="inward",
-    )(send2, brecv)
-    hres, hsend = pl.pallas_call(
-        term_kernel, out_shape=(sds(2, 8, 3072), sds(8, 2, 8, 384)), in_specs=[VM] * 6, out_specs=(VM, VM),
-        scratch_shapes=[pltpu.VMEM((512, 128), F32), pltpu.VMEM((NPAIR, 16, 128), F32)],
-        compiler_params=params(), name="term",
-    )(recv2, res, gm, sc, w["vza"], w["vzb"])
-    tile = pl.pallas_call(
-        late_kernel, out_shape=sds(8, 128), in_specs=[VM] * 3, out_specs=VM,
-        scratch_shapes=[
-            pltpu.VMEM((2, 64, 384), F32), pltpu.VMEM((512, 768), F32), pltpu.VMEM((64, 768), F32),
-            pltpu.VMEM((96, 768), F32), pltpu.VMEM((8, 48, 128), F32), pltpu.VMEM((8, 48, 128), F32),
-            pltpu.VMEM((256, 128), F32), pltpu.VMEM((256, 128), F32),
-            DMA((NBD,)), DMA((NBD,)), DMA((NBD,)), DMA((NBD,)), DMA((NF,)), DMA((NF,))],
-        compiler_params=params(collective_id=2, has_side_effects=True), name="late",
-    )(hsend, brecv, early)
+            vm(2, 8, 3072), vm(2, 8, 3072), vm(2, 8, 3072), vm(2, 8, 3072), vi(1, 3072), vi(NF, 128), vm(3, L, L),
+            v16(384, 192), v16(384, 256), v16(192, 224), v16(192, 112), v16(224, 192), v16(256, 256), v16(128, 192),
+            v16(128, 96), vm(2, 8, 3072),
+            vm(16, 3072), vm(768, 128), vm(8, 10, 8, 384), vm(24, 16, 128), vi(64, 128), v16(64, 3072),
+            v16(128, 3072), vm(512, 128),
+            vm(768, 128), vm(10, 64, 384), v16(64, 2048), v16(128, 2048), vi(64, 128), vi(32, 128), vm(3, L, 128),
+            vm(16, 48, 128), vm(1200, 128), vm(2, 1344, 128), vm(1344, 128), vm(NPAIR, 48, 128), vm(768, 128),
+            vm(768, 128),
+            vm(512, 768), vm(192, 768), vm(512, 768), vm(8, 256, 128), vm(8, 256, 128), vm(512, 128),
+            vm(NPAIR, 16, 128), vm(8, 2, 8, 384), vm(2, 64, 384), vm(96, 768), vm(8, 48, 128), vm(8, 48, 128),
+            vm(256, 128), vm(256, 128)] + sems + [DMA((16,))],
+        compiler_params=pltpu.CompilerParams(collective_id=0, has_side_effects=True, vmem_limit_bytes=BIG), name="step",
+    )(eigen_values, current, h_current, previous, h_previous, gm, sc, potential,
+      w["wz"], w["wy"], w["wxa"], w["wxb"], w["vx"], w["vy"], w["vza"], w["vzb"])
     mats = jnp.transpose(tile[0:6].reshape(6, 4, 32)[:, :, 0:24], (1, 2, 0))
     return hres, mats[0:2], mats[2:4]
 

time: 103 us -> 82.6 us (0.80)
  Pallas kernels: 93.7 us -> 77.4 us
  local copies, waits for them, and re-layouts: 7.46 us -> 2.98 us
    pallas_call x6 -> x1, Pallas kernels: 93.7 us -> 77.4 us  [local(): pl.pallas_call(step_kernel, out_shape=(sds(2, 8, 3072), sds(8, 128)), in_...]
    unnamed x36 -> x3, local copies, waits for them, and re-layouts: 6.77 us -> 2.29 us
where the time goes in v2:
time: 82.6 us; the launch traced here: 81.1 us
  Pallas kernels  77.4 us (94%)
  local copies, waits for them, and re-layouts  2.98 us (4%)
    pallas_call x1, Pallas kernels, local(): pl.pallas_call(step_kernel, out_shape=(sds(2, 8, 3072), sds(8, 128)), in_...  77.4 us
    unnamed x3, local copies, waits for them, and re-layouts  2.29 us

profile of v2, /device:TPU:4, one launch (start us, length us, event | category | flops | bytes accessed | tf_op | source)
XLA Modules:
  0.0 81.1 jit_solution(7204770897811684230)
XLA Ops:
  0.6 77.4 %step.1 = (f32[2,8,3072]{2,1,0:T(8,128)}, f32[8,128]{1,0:T(8,128)}) custom-call(f32[8]{0:T(128)} %ev.1, f32[2,8,3072]{2,1,0:T(8,128)} %cur_h.1, f32[2,8,3072]{2,1,0:T(8,128)} %hcur_h.1, f32[2,8,3072]{2,1,0:T(8,128)} %prev_h.1, f32[2,8,3072]{2,1,0:T(8,128)} %hprev_h.1, s32[1,3072]{1,0:T(1,128)} %bitcast.6, s32[32,128]{1,0:T(8,128)} %bitcast.5, ...), custom_call_target="tpu_custom_call" | custom-call | tf_op jit(solution)/shard_map/step/pallas_call | solution.py:565
  78.1 0.0 copy-start
  78.1 0.7 copy-done
  78.8 0.1 reshape.17
  78.9 0.6 fusion
  79.5 1.6 %copy.20 = f32[2,8,3072]{2,1,0:T(8,128)} copy(f32[2,8,3072]{2,1,0:T(8,128)} %get-tuple-element.12) | data formatting | bytes 393216
  (1 shorter events, 0.0 us)
Async XLA Ops:
  78.1 0.7 copy-start

commit v3 on v2

v3 whole, which is shorter than its diff:
```python
import math

import jax
import jax.numpy as jnp
import ml_dtypes
import numpy as np
from jax import lax
from jax.experimental import pallas as pl
from jax.experimental.pallas import tpu as pltpu
from jax.sharding import PartitionSpec as P

L = 96
CUT = 24
F32 = jnp.float32
BF16 = jnp.bfloat16
NF = 32
NBD = 8
GT = 24
NT = 13
MESH = pl.DeviceIdType.MESH
VM = pl.BlockSpec(memory_space=pltpu.VMEM)
HB = pl.BlockSpec(memory_space=pltpu.HBM)
SM = pl.BlockSpec(memory_space=pltpu.SMEM)


def split_np(table):
    high = table.astype(ml_dtypes.bfloat16)
    low = (table - high.astype(np.float64)).astype(ml_dtypes.bfloat16)
    return high, low


def tables():
    zout = (np.arange(NF)[None, :] * 3 + np.arange(3)[:, None]).reshape(-1)
    wz = np.zeros((2, 2, L, 2, 32))
    for par in range(2):
        zi = 2 * np.arange(32) + par
        ok = zi <= 2 * CUT
        ang = 2 * math.pi / L * ((zout[:, None] * (zi - CUT)[None, :]) % L)
        c, s = np.cos(ang) * ok, np.sin(ang) * ok
        wz[par, 0, :, 0], wz[par, 0, :, 1] = c, -s
        wz[par, 1, :, 0], wz[par, 1, :, 1] = s, c
    zh, zl = split_np(wz.reshape(384, 64))
    wz = np.concatenate([zh, zh, zl], axis=1)
    n = np.arange(L)
    k = np.arange(49) - CUT
    ang = 2 * math.pi / L * ((k[:, None] * n[None, :]) % L)
    c, s = np.cos(ang), np.sin(ang)
    wy = np.zeros((2, 64, 2, 128))
    wy[0, :49, 0, :L], wy[0, :49, 1, :L] = c, s
    wy[1, :49, 0, :L], wy[1, :49, 1, :L] = -s, c
    yh, yl = split_np(wy.reshape(128, 256))
    wy = np.concatenate([yh, yh, yl], axis=0)
    wx = np.zeros((2, L, 2, 56))
    wx[0, :, 0, :49], wx[0, :, 1, :49] = c.T, -s.T
    wx[1, :, 0, :49], wx[1, :, 1, :49] = s.T, c.T
    xh, xl = split_np(wx.reshape(192, 112))
    wx = np.concatenate([xh, xh, xl], axis=1)
    vx = np.zeros((2, 56, 2, L))
    vx[0, :49, 0], vx[0, :49, 1] = c, s
    vx[1, :49, 0], vx[1, :49, 1] = -s, c
    vh, vl = split_np(vx.reshape(112, 192))
    vx = np.concatenate([vh, vh, vl], axis=1)
    vy = np.zeros((2, 128, 2, 64))
    vy[0, :L, 0, :49], vy[0, :L, 1, :49] = c.T, -s.T
    vy[1, :L, 0, :49], vy[1, :L, 1, :49] = s.T, c.T
    vyh, vyl = split_np(vy.reshape(256, 128))
    vy = np.concatenate([vyh, vyl], axis=1)
    vz = np.zeros((2, 64, L))
    ang = 2 * math.pi / L * ((k[:, None] * zout[None, :]) % L)
    vz[0, :49], vz[1, :49] = np.cos(ang), np.sin(ang)
    zbh, zbl = split_np(vz.reshape(128, L))
    vz = np.concatenate([zbh, zbh, zbl], axis=1)
    return dict(wz=wz, wy=wy, wx=wx, vx=vx, vy=vy, vz=vz)


def dot(a, b):
    return jnp.dot(a, b, preferred_element_type=F32)


def dot_nt(a, b):
    return lax.dot_general(a, b, (((1,), (1,)), ((), ())), preferred_element_type=F32)


def halves(x):
    hi = x.astype(BF16)
    return hi, (x - hi.astype(F32)).astype(BF16)


def low_lanes(shape):
    return lax.broadcasted_iota(jnp.int32, shape, len(shape) - 1) < 64


def swap(x):
    return pltpu.roll(x, 64, 1)


def div96(v):
    return (v * 43691) >> 22


def signed(v):
    return jnp.where(v >= L // 2, v - L, v)


def lanes_of(x, index):
    return jnp.take_along_axis(x, index, axis=1, mode="promise_in_bounds")


def slot_facts(m, cols):
    live = m >= 0
    ms = jnp.maximum(m, 0)
    slot = div96(ms)
    z = signed(ms - slot * L)
    col = jnp.where(live, lanes_of(cols, slot), 0)
    xc = div96(col)
    x = signed(xc)
    y = signed(col - xc * L)
    norm = x * x + y * y + z * z
    kin = jnp.where(live, 64.0 * norm.astype(F32) / float(L * L), 0.0)
    zi = z + CUT
    four = jnp.where(live, zi >> 2, -1)
    lane = jnp.where(live, (zi & 3) * 64 + slot - 64, -1)
    return live, kin, four, lane


def one_hot_rows(key, rows):
    return jnp.where(jnp.broadcast_to(key, (256, 128)) == rows, 1.0, 0.0).astype(BF16)


def four_masks(four):
    wide = jnp.broadcast_to(four, (16, 128))
    return [jnp.where(wide == t, 1.0, 0.0).astype(BF16) for t in range(NT)]


def residual(ev, cur, hcur, gm, scols, res, lhs, hit, kinr, fourr, liver):
    me = lax.axis_index("fft")
    cols = jnp.broadcast_to(scols[pl.ds(me, 1), :], (8, 128))
    row = lax.broadcasted_iota(jnp.int32, (8, 128), 0)
    evc = jnp.zeros((8, 128), F32)
    for b in range(8):
        evc = jnp.where(row == b, ev[b], evc)
    rows = lax.broadcasted_iota(jnp.int32, (256, 128), 0)

    for k in range(GT):
        at = pl.ds(128 * k, 128)
        live, kin, four, lane = slot_facts(jnp.broadcast_to(gm[:, at], (8, 128)), cols)
        kinr[:, at] = kin
        fourr[:, at] = four
        liver[:, at] = live.astype(F32)
        den = 1.0 + kin
        r = jnp.concatenate(
            [jnp.where(live, (hcur[c, :, at] - evc * cur[c, :, at]) / den, 0.0) for c in range(2)], axis=0)
        res[:, at] = r
        hi, lo = halves(r)
        hit[:, at] = one_hot_rows(lane[:1], rows)
        for t, m in enumerate(four_masks(four[:1])):
            lhs[32 * t : 32 * t + 16, at] = hi * m
            lhs[32 * t + 16 : 32 * t + 32, at] = lo * m


def sticks(lhs, hit, wz, send, y):
    out = dot_nt(lhs[...], hit[...])
    y[416:512, :] = jnp.zeros((96, 128), F32)
    for t in range(NT):
        o = out[32 * t : 32 * t + 16] + out[32 * t + 16 : 32 * t + 32]
        for h in range(2):
            y[32 * t + 16 * h : 32 * t + 16 * h + 16, :] = o[:, 128 * h : 128 * h + 128]
    low = low_lanes((192, 128))
    low96 = low_lanes((96, 128))
    parts = []
    for b in range(8):
        x = jnp.concatenate([y[pl.ds(c * 8 + b, 32, stride=16), :] for c in range(2)], axis=0)
        hi, lo = halves(x)
        parts.append(jnp.concatenate([hi, lo, hi], axis=0))
    out = dot(wz[...], jnp.concatenate(parts, axis=1))
    for b in range(8):
        o = out[:, 128 * b : 128 * b + 128]
        w = jnp.where(low, o[:192], o[192:])
        w = w + swap(w)
        w = jnp.where(low96, w[:96], w[96:])
        for zl in range(3):
            send[pl.ds(256 * zl + b, 32, stride=8), :] = w[32 * zl : 32 * zl + 32]


def basis_rows(cur, hcur, prev, hprev, res, liver, bsend):
    def tile(d, carry):
        at = pl.ds(pl.multiple_of(384 * d, 128), 384)
        live = liver[:, at] > 0.0
        for c in range(2):
            bsend[d, c] = jnp.where(live, cur[c, :, at], 0.0)
            bsend[d, 2 + c] = res[8 * c : 8 * c + 8, at]
            bsend[d, 4 + c] = jnp.where(live, prev[c, :, at], 0.0)
            bsend[d, 6 + c] = jnp.where(live, hcur[c, :, at], 0.0)
            bsend[d, 8 + c] = jnp.where(live, hprev[c, :, at], 0.0)
        return carry

    lax.fori_loop(0, NBD, tile, 0)


def greet_everyone():
    f, b = lax.axis_index("fft"), lax.axis_index("band")
    barrier = pltpu.get_barrier_semaphore()

    def greet(i, c):
        pl.semaphore_signal(barrier, inc=1, device_id=(b, lax.rem(f + i, NF)), device_id_type=MESH)
        return c

    def greet_b(i, c):
        pl.semaphore_signal(barrier, inc=1, device_id=(lax.rem(b + i, NBD), f), device_id_type=MESH)
        return c

    lax.fori_loop(1, NF, greet, 0)
    lax.fori_loop(1, NBD, greet_b, 0)


def everyone_in():
    pl.semaphore_wait(pltpu.get_barrier_semaphore(), NF - 1 + NBD - 1)


FAR_FIRST = sorted(
    [(dx, dz) for dx in range(4) for dz in range(8) if dx or dz], key=lambda o: -min(o[0], 4 - o[0]) - min(o[1], 8 - o[1]))


def whole(ref, sem):
    pltpu.make_async_copy(ref, ref, sem).wait()


class FftExchange:
    def __init__(self, src, dst, ssem, rsem):
        self.a = (src, dst, ssem, rsem)

    def start(self, g=0):
        src, dst, ssem, rsem = self.a
        f, b = lax.axis_index("fft"), lax.axis_index("band")
        to_me = dst.at[pl.ds(pl.multiple_of(256 * g + 8 * f, 8), 8), :]

        for dx, dz in FAR_FIRST:
            to = lax.rem(f // 8 + dx, 4) * 8 + lax.rem(f + dz, 8)
            pltpu.make_async_remote_copy(
                src_ref=src.at[pl.ds(pl.multiple_of(256 * g + 8 * to, 8), 8), :], dst_ref=to_me,
                send_sem=ssem.at[g], recv_sem=rsem.at[g], device_id=(b, to), device_id_type=MESH).start()
        own = src.at[pl.ds(pl.multiple_of(256 * g + 8 * f, 8), 8), :]
        pltpu.make_async_copy(own, to_me, rsem.at[g]).start()

    def wait(self, g=0):
        src, dst, ssem, rsem = self.a
        whole(dst.at[pl.ds(pl.multiple_of(256 * g, 256), 256), :], rsem.at[g])

    def sent(self, g=0):
        src, dst, ssem, rsem = self.a
        whole(src.at[pl.ds(256 * g, 248), :], ssem.at[g])


class BandExchange:
    def __init__(self, src, dst, place, ssem, rsem):
        self.a = (src, dst, place, ssem, rsem)

    def start(self):
        src, dst, place, ssem, rsem = self.a
        f, b = lax.axis_index("fft"), lax.axis_index("band")
        for i in range(1, NBD):
            to = lax.rem(b + i, NBD)
            pltpu.make_async_remote_copy(
                src_ref=src.at[to], dst_ref=place(dst, b), send_sem=ssem, recv_sem=rsem,
                device_id=(to, f), device_id_type=MESH).start()
        pltpu.make_async_copy(src.at[b], place(dst, b), rsem).start()

    def wait(self):
        src, dst, place, ssem, rsem = self.a
        whole(dst, rsem)

    def sent(self):
        src, dst, place, ssem, rsem = self.a
        whole(src.at[pl.ds(0, NBD - 1)], ssem)


class BandSum:
    def __init__(self, src, got, mid, dst, sems):
        self.a = (src, got, mid, dst, sems)
        b = lax.axis_index("band")
        self.y, self.c = b // 2, lax.rem(b, 2)

    def first(self):
        src, got, mid, dst, sems = self.a
        pltpu.make_async_remote_copy(
            src_ref=src.at[1 - self.c], dst_ref=got, send_sem=sems.at[0], recv_sem=sems.at[1],
            device_id=(2 * self.y + 1 - self.c, lax.axis_index("fft")), device_id_type=MESH).start()

    def second(self):
        src, got, mid, dst, sems = self.a
        whole(got, sems.at[1])
        mid[...] = src[self.c] + got[...]
        for i in (2, 1, 3):
            to = lax.rem(self.y + i, 4)
            pltpu.make_async_remote_copy(
                src_ref=mid.at[to], dst_ref=dst.at[self.y], send_sem=sems.at[2], recv_sem=sems.at[3],
                device_id=(2 * to + self.c, lax.axis_index("fft")), device_id_type=MESH).start()
        pltpu.make_async_copy(mid.at[self.y], dst.at[self.y], sems.at[3]).start()

    def total(self):
        src, got, mid, dst, sems = self.a
        whole(dst, sems.at[3])
        return (dst[0] + dst[1]) + (dst[2] + dst[3])

    def sent(self):
        src, got, mid, dst, sems = self.a
        whole(got, sems.at[0])
        whole(mid.at[pl.ds(0, 3)], sems.at[2])


def band_rows(dst, frm):
    return dst.at[:, pl.ds(pl.multiple_of(frm * 8, 8), 8), :]


def plane_maps(scols, pot, hit, mask, fourr, potp):
    low1 = low_lanes((1, 128))
    rows = lax.broadcasted_iota(jnp.int32, (256, 128), 0)
    for k in range(16):
        col = jnp.where(low1, swap(scols[2 * k : 2 * k + 1, :]), scols[2 * k + 1 : 2 * k + 2, :])
        live = col >= 0
        colp = jnp.maximum(col, 0)
        xc = div96(colp)
        xi = signed(xc) + CUT
        yi = signed(colp - xc * L) + CUT
        four = jnp.where(live, xi >> 2, -1)
        at = pl.ds(128 * k, 128)
        fourr[:, at] = jnp.broadcast_to(four, (8, 128))
        hit[:, at] = one_hot_rows(jnp.where(live, (xi & 3) * 64 + yi, -1), rows)
        for t, m in enumerate(four_masks(four)):
            mask[16 * t : 16 * t + 16, at] = m
    potp[...] = jnp.zeros((3, L, 128), F32)
    potp[:, :, 0:L] = pot[...]


def place(g, recv, hit, mask, lhs, pm):
    low = low_lanes((8, 128))
    for k in range(16):
        at = pl.ds(128 * k, 128)
        base = pl.multiple_of(256 * g + 16 * k, 16)
        r0, r1 = recv[pl.ds(base, 8), :], recv[pl.ds(base + 8, 8), :]
        hi, lo = halves(jnp.concatenate([jnp.where(low, r0, swap(r1)), jnp.where(low, swap(r0), r1)], axis=0))
        for t in range(NT):
            m = mask[16 * t : 16 * t + 16, at]
            lhs[32 * t : 32 * t + 16, at] = hi * m
            lhs[32 * t + 16 : 32 * t + 32, at] = lo * m
    out = dot_nt(lhs[...], hit[...])
    for t in range(NT):
        o = out[32 * t : 32 * t + 16] + out[32 * t + 16 : 32 * t + 32]
        for h in range(2):
            re, im = o[:8, 128 * h : 128 * h + 128], o[8:, 128 * h : 128 * h + 128]
            base = 32 * t + 16 * h
            pm[base : base + 8, :] = jnp.where(low, re, swap(im))
            pm[base + 8 : base + 16, :] = jnp.where(low, swap(re), im)


def along_y(pm, wy, tt):
    hi, lo = halves(pm[0:416, :])
    out = dot(jnp.concatenate([hi, lo], axis=1), wy[0:256, :]) + dot(hi, wy[256:384, :])
    tt[0, 0:416, :] = out[:, 0:128]
    tt[1, 0:416, :] = out[:, 128:256]
    tt[:, 416:448, :] = jnp.zeros((2, 32, 128), F32)


def along_x(g, tt, potp, wx, vx, vy, gg):
    pv = potp[g]
    pv = jnp.concatenate([pv] * 8, axis=1)
    pv = jnp.concatenate([pv, pv], axis=0)
    his, los = [], []
    for b in range(8):
        hi, lo = halves(jnp.concatenate([tt[c, pl.ds(b, 56, stride=8), :] for c in range(2)], axis=0))
        his.append(hi)
        los.append(lo)
    hi = jnp.concatenate(his, axis=1)
    u = dot(wx[...], jnp.concatenate([hi, jnp.concatenate(los, axis=1), hi], axis=0))
    hi, lo = halves(u * pv)
    t = dot(vx[...], jnp.concatenate([hi, lo, hi], axis=0))
    hi, lo = halves(jnp.concatenate(
        [jnp.concatenate([t[56 * c : 56 * c + 56, 128 * b : 128 * b + 128] for c in range(2)], axis=1) for b in range(8)],
        axis=0))
    a = dot(hi, vy[...])
    q = a[:, 0:128] + a[:, 128:256] + dot(lo, vy[:, 0:128])
    for b in range(8):
        gg[pl.ds(b, 56, stride=8), :] = q[56 * b : 56 * b + 56]


def fours(src, low):
    blocks = []
    for t in range(NT):
        cols = []
        for h in range(2):
            base = 32 * t + 16 * h
            g0, g1 = src[base : base + 8, :], src[base + 8 : base + 16, :]
            cols.append(jnp.concatenate([jnp.where(low, g0, swap(g1)), jnp.where(low, swap(g0), g1)], axis=0))
        blocks.append(jnp.concatenate(cols, axis=1))
    hi, lo = halves(jnp.concatenate(blocks, axis=0))
    return jnp.concatenate([hi, lo], axis=1)


def pick(lhs, hit, fourr, n, width):
    at = pl.ds(n * width, width)
    d = hit[:, at]
    out = dot(lhs, jnp.concatenate([d, d], axis=0))
    f = fourr[:, at]
    f = jnp.concatenate([f, f], axis=0)
    acc = jnp.zeros((16, width), F32)
    for t in range(NT):
        acc = jnp.where(f == t, out[16 * t : 16 * t + 16], acc)
    return acc


def collect(g, gg, hit, fourr, gl, send):
    low = low_lanes((8, 128))
    gl[...] = fours(gg, low)
    for n in range(8):
        acc = pick(gl[...], hit, fourr, n, 256)
        for k in range(2):
            re, im = acc[0:8, 128 * k : 128 * k + 128], acc[8:16, 128 * k : 128 * k + 128]
            base = pl.multiple_of(256 * g + 32 * n + 16 * k, 16)
            send[pl.ds(base, 8), :] = jnp.where(low, re, swap(im))
            send[pl.ds(base + 8, 8), :] = jnp.where(low, swap(re), im)


def row_side(brecv, qs):
    zero = jnp.zeros((8, 768), F32)
    for d in range(NBD):
        for j in range(3):
            g8 = 3 * d + j
            ty, r0 = g8 // 8, (g8 % 8) * 8
            re, im = brecv[2 * ty, r0 : r0 + 8, :], brecv[2 * ty + 1, r0 : r0 + 8, :]
            o = 64 * d + 8 * j
            qs[o : o + 8, 0:384] = re
            qs[o : o + 8, 384:768] = im
            qs[o + 32 : o + 40, 0:384] = -im
            qs[o + 32 : o + 40, 384:768] = re
        qs[64 * d + 24 : 64 * d + 32, :] = zero
        qs[64 * d + 56 : 64 * d + 64, :] = zero


def early_gram(brecv, qs, flat, ks, esend):
    for m in range(2):
        for ty in range(3):
            at = 64 * ty
            if m == 1 and ty == 1:
                flat[at : at + 64, :] = jnp.zeros((64, 768), F32)
                continue
            src = 2 * ty if m == 0 else (6 if ty == 0 else 8)
            flat[at : at + 64, 0:384] = brecv[src]
            flat[at : at + 64, 384:768] = brecv[src + 1]
        ks[256 * m : 256 * m + 256, :] = jnp.zeros((256, 768), F32)
        for f in range(NF):
            ks[256 * m + 8 * f : 256 * m + 8 * f + 6, :] = flat[6 * f : 6 * f + 6, :]
    khi, klo = halves(ks[...])
    low = low_lanes((256, 128))
    for n in range(2):
        qhi, qlo = halves(qs[256 * n : 256 * n + 256, :])
        g = dot_nt(khi, qhi) + dot_nt(klo, qhi) + dot_nt(khi, qlo)
        for j in range(2):
            c, h = g[0:256, 128 * j : 128 * j + 128], g[256:512, 128 * j : 128 * j + 128]
            esend[0, 2 * n + j] = jnp.where(low, c, swap(h))
            esend[1, 2 * n + j] = jnp.where(low, swap(c), h)

def term(recv, res, hit, fourr, kinr, liver, vz, hres, hsend, z, zl_):
    his, los = [], []
    for b in range(8):
        hi, lo = halves(jnp.concatenate([recv[pl.ds(256 * zl + b, 32, stride=8), :] for zl in range(3)], axis=0))
        his.append(hi)
        los.append(lo)
    hi = jnp.concatenate(his, axis=1)
    out = dot(vz[...], jnp.concatenate([hi, jnp.concatenate(los, axis=1), hi], axis=0))
    low = low_lanes((64, 128))
    for b in range(8):
        o = out[:, 128 * b : 128 * b + 128]
        other = swap(o[64:128])
        z[pl.ds(b, 64, stride=8), :] = o[0:64] + jnp.where(low, other, -other)
    zl_[...] = fours(z, low_lanes((8, 128)))
    for n in range(12):
        at = pl.ds(256 * n, 256)
        acc = pick(zl_[...], hit, fourr, n, 256)
        live = liver[:, at] > 0.0
        for c in range(2):
            v = kinr[:, at] * res[8 * c : 8 * c + 8, at] + acc[8 * c : 8 * c + 8] * (1.0 / float(L**3))
            v = jnp.where(live, v, 0.0)
            hres[c, :, at] = v
            for k in range(2):
                q = 2 * n + k
                hsend[q // 3, c, :, (q % 3) * 128 : (q % 3) * 128 + 128] = v[:, 128 * k : 128 * k + 128]


F0, F1 = 10, 22


def late_gram(hrecv, qs, flat, ks, lsend):
    ks[...] = jnp.zeros((96, 768), F32)
    flat[0:64, 0:384] = hrecv[0]
    flat[0:64, 384:768] = hrecv[1]
    for f in range(F0, F1):
        k0, k1 = max(6 * f, 64), min(6 * f + 6, 128)
        o = 8 * (f - F0) + k0 - 6 * f
        ks[o : o + k1 - k0, :] = flat[k0 - 64 : k1 - 64, :]
    khi, klo = halves(ks[...])
    low = low_lanes((48, 128))
    for n in range(2):
        qhi, qlo = halves(qs[256 * n : 256 * n + 256, :])
        g = dot_nt(khi, qhi) + dot_nt(klo, qhi) + dot_nt(khi, qlo)
        for j in range(2):
            a, b = g[0:48, 128 * j : 128 * j + 128], g[48:96, 128 * j : 128 * j + 128]
            lsend[0, 2 * n + j] = jnp.where(low, a, swap(b))
            lsend[1, 2 * n + j] = jnp.where(low, swap(a), b)


def step_kernel(ev, cur_h, hcur_h, prev_h, hprev_h, gm_h, scols_h, pot_h, wz_h, wy_h, wx_h, vx_h, vy_h,
                vz_h, hres_h, out,
                cur, hcur, prev, hprev, gm, scols, pot, wz, wy, wx, vx, vy, vz, hres,
                res, kinr, gfour, liver, ghit, glhs, y, send, bsend,
                recv, brecv, shit, smask, sfour, slhs, potp, pm, tt, gg, gl, send2, recv2,
                qs, flat, ks, esend, egot, emid, erecv, z, zl, hsend, hrecv, lks,
                lsend, lgot, lmid, lrecv, fsend, frecv, s1, r1, s3, r3, s4, s6, sems, load):
    pairs = [(gm_h, gm), (scols_h, scols), (cur_h, cur), (hcur_h, hcur), (wz_h, wz), (prev_h, prev), (hprev_h, hprev),
             (pot_h, pot), (wy_h, wy), (wx_h, wx), (vx_h, vx), (vy_h, vy), (vz_h, vz)]
    loads = [pltpu.make_async_copy(a, b, load.at[i]) for i, (a, b) in enumerate(pairs)]
    for copy in loads:
        copy.start()
    greet_everyone()
    for copy in loads[:5]:
        copy.wait()
    x1 = FftExchange(send, recv, s1, r1)
    x2 = BandExchange(bsend, brecv, band_rows, sems.at[0], sems.at[1])
    x3 = FftExchange(send2, recv2, s3, r3)
    x4 = BandSum(esend, egot, emid, erecv, s4)
    x5 = BandExchange(hsend, hrecv, band_rows, sems.at[4], sems.at[5])
    x6 = BandSum(lsend, lgot, lmid, lrecv, s6)
    x7 = FftExchange(fsend, frecv, sems.at[pl.ds(8, 1)], sems.at[pl.ds(9, 1)])
    residual(ev, cur, hcur, gm, scols, res, glhs, ghit, kinr, gfour, liver)
    sticks(glhs, ghit, wz, send, y)
    everyone_in()
    for g in range(3):
        x1.start(g)
    for copy in loads[5:]:
        copy.wait()
    basis_rows(cur, hcur, prev, hprev, res, liver, bsend)
    plane_maps(scols, pot, shit, smask, sfour, potp)

    def plane(g, carry):
        x1.wait(g)
        pl.when(g == 0)(x2.start)
        place(g, recv, shit, smask, slhs, pm)
        along_y(pm, wy, tt)
        along_x(g, tt, potp, wx, vx, vy, gg)
        collect(g, gg, shit, sfour, gl, send2)
        x3.start(g)
        return carry

    lax.fori_loop(0, 3, plane, 0)
    x2.wait()
    row_side(brecv, qs)
    early_gram(brecv, qs, flat, ks, esend)
    x4.first()
    x4.second()
    for g in range(3):
        x3.wait(g)
    term(recv2, res, ghit, gfour, kinr, liver, vz, hres, hsend, z, zl)
    x5.start()
    store = pltpu.make_async_copy(hres, hres_h, load.at[15])
    store.start()
    fsend[...] = x4.total()
    x5.wait()
    late_gram(hrecv, qs, flat, lks, lsend)
    x6.first()
    x6.second()
    low = low_lanes((48, 128))
    total = x6.total()
    fsend[8 * F0 : 8 * F0 + 48, :] = fsend[8 * F0 : 8 * F0 + 48, :] + jnp.where(low, 0.0, swap(total))
    fsend[8 * F0 + 48 : 8 * F0 + 96, :] = fsend[8 * F0 + 48 : 8 * F0 + 96, :] + jnp.where(low, 0.0, total)
    x7.start()
    x7.wait()
    total = frecv[0:8, :]
    for d in range(1, NF):
        total = total + frecv[8 * d : 8 * d + 8, :]
    out[...] = total * (8.0 / float(L**3))
    store.wait()
    for g in range(3):
        x1.sent(g)
        x3.sent(g)
    for x in (x2, x4, x5, x6, x7):
        x.sent()


def sds(*shape):
    return jax.ShapeDtypeStruct(shape, F32)


DMA = pltpu.SemaphoreType.DMA
BIG = 64 * 1024 * 1024


def local(current, h_current, previous, h_previous, eigen_values, potential, stick_cols, g_map):
    w = tables()
    gm = g_map.reshape(1, 3072)
    sc = stick_cols.reshape(NF, 128)
    vm = lambda *shape: pltpu.VMEM(shape, F32)
    v16 = lambda *shape: pltpu.VMEM(shape, BF16)
    vi = lambda *shape: pltpu.VMEM(shape, jnp.int32)
    hres, tile = pl.pallas_call(
        step_kernel, out_shape=(sds(2, 8, 3072), sds(8, 128)), in_specs=[SM] + [HB] * 13, out_specs=(HB, VM),
        scratch_shapes=[
            vm(2, 8, 3072), vm(2, 8, 3072), vm(2, 8, 3072), vm(2, 8, 3072), vi(1, 3072), vi(NF, 128), vm(3, L, L),
            v16(384, 192), v16(384, 256), v16(192, 336), v16(112, 576), v16(256, 256), v16(128, 288),
            vm(2, 8, 3072),
            vm(16, 3072), vm(8, 3072), vi(8, 3072), vm(8, 3072), v16(256, 3072), v16(416, 3072), vm(512, 128),
            vm(768, 128), vm(8, 10, 8, 384),
            vm(768, 128), vm(10, 64, 384), v16(256, 2048), v16(208, 2048), vi(8, 2048), v16(416, 2048),
            vm(3, L, 128), vm(416, 128), vm(2, 448, 128), vm(448, 128), v16(208, 512), vm(768, 128), vm(768, 128),
            vm(512, 768), vm(192, 768), vm(512, 768), vm(2, 4, 256, 128), vm(4, 256, 128), vm(4, 256, 128),
            vm(4, 256, 128), vm(512, 128),
            v16(208, 512), vm(8, 2, 8, 384), vm(2, 64, 384), vm(96, 768), vm(2, 4, 48, 128), vm(4, 48, 128), vm(4, 48, 128), vm(4, 48, 128),
            vm(256, 128), vm(256, 128), DMA((3,)), DMA((3,)), DMA((3,)), DMA((3,)), DMA((4,)), DMA((4,)), DMA((10,)), DMA((16,))],
        compiler_params=pltpu.CompilerParams(collective_id=0, has_side_effects=True, vmem_limit_bytes=BIG), name="step",
    )(eigen_values, current, h_current, previous, h_previous, gm, sc, potential,
      w["wz"], w["wy"], w["wx"], w["vx"], w["vy"], w["vz"])
    mats = jnp.transpose(tile[0:6].reshape(6, 4, 32)[:, :, 0:24], (1, 2, 0))
    return hres, mats[0:2], mats[2:4]


def solution(mesh):
    bf = P(None, "band", "fft")
    in_specs = (bf, bf, bf, bf, P("band"), P("fft", None, None), P(), P("fft"))
    return jax.shard_map(local, mesh=mesh, in_specs=in_specs, out_specs=(bf, bf, bf), check_vma=False)
```

time: 82.6 us -> 59.3 us (0.72)
  the two profiles are of different devices: /device:TPU:4 before, /device:TPU:8 now
where the time goes in v3:
time: 59.3 us; the launch traced here: 59.1 us
  Pallas kernels  55.5 us (94%)
  local copies, waits for them, and re-layouts  2.98 us (5%)
  between operations  0.65 us (1%)
    pallas_call x1, Pallas kernels, local(): pl.pallas_call(step_kernel, out_shape=(sds(2, 8, 3072), sds(8, 128)), in_...  55.5 us
    unnamed x3, local copies, waits for them, and re-layouts  2.29 us

profile of v3, /device:TPU:8, one launch (start us, length us, event | category | flops | bytes accessed | tf_op | source)
XLA Modules:
  0.0 59.1 jit_solution(8142299854099025995)
XLA Ops:
  0.6 55.5 %step.1 = (f32[2,8,3072]{2,1,0:T(8,128)}, f32[8,128]{1,0:T(8,128)}) custom-call(f32[8]{0:T(128)} %ev.1, f32[2,8,3072]{2,1,0:T(8,128)} %cur_h.1, f32[2,8,3072]{2,1,0:T(8,128)} %hcur_h.1, f32[2,8,3072]{2,1,0:T(8,128)} %prev_h.1, f32[2,8,3072]{2,1,0:T(8,128)} %hprev_h.1, s32[1,3072]{1,0:T(1,128)} %bitcast.6, s32[32,128]{1,0:T(8,128)} %bitcast.5, ...), custom_call_target="tpu_custom_call" | custom-call | tf_op jit(solution)/shard_map/step/pallas_call | solution.py:603
  56.1 0.0 copy-start
  56.2 0.7 %copy-done = f32[8,128]{1,0:T(8,128)S(1)} copy-done((f32[8,128]{1,0:T(8,128)S(1)}, f32[8,128]{1,0:T(8,128)}, u32[]{:S(2)}) %copy-start) | copy-done | bytes 4120
  56.8 0.1 reshape.17
  56.9 0.6 %fusion = (f32[2,24,6]{1,0,2:T(2,128)}, f32[2,24,6]{1,0,2:T(2,128)}) fusion(f32[4,24,6]{1,0,2:T(4,128)S(1)} %slice_bitcast_fusion), kind=kLoop, calls=%fused_computation.1 | loop fusion | bytes 4608 | tf_op jit(solution)/shard_map/slice | solution.py:621
  57.5 1.6 %copy.18 = f32[2,8,3072]{2,1,0:T(8,128)} copy(f32[2,8,3072]{2,1,0:T(8,128)} %get-tuple-element.12) | data formatting | bytes 393216
  (1 shorter events, 0.0 us)
Async XLA Ops:
  56.1 0.7 %copy-start = (f32[8,128]{1,0:T(8,128)S(1)}, f32[8,128]{1,0:T(8,128)}, u32[]{:S(2)}) copy-start(f32[8,128]{1,0:T(8,128)} %get-tuple-element.6) | copy-start | bytes 12292

commit v4 on v3

--- a/solution.py
+++ b/solution.py
@@ -427,7 +427,7 @@
             g8 = 3 * d + j
             ty, r0 = g8 // 8, (g8 % 8) * 8
             re, im = brecv[2 * ty, r0 : r0 + 8, :], brecv[2 * ty + 1, r0 : r0 + 8, :]
-            o = 64 * d + 8 * j
+            o = 64 * (4 * (d % 2) + d // 2) + 8 * j
             qs[o : o + 8, 0:384] = re
             qs[o : o + 8, 384:768] = im
             qs[o + 32 : o + 40, 0:384] = -im
@@ -436,28 +436,22 @@
         qs[64 * d + 56 : 64 * d + 64, :] = zero
 
 
-def early_gram(brecv, qs, flat, ks, esend):
-    for m in range(2):
-        for ty in range(3):
-            at = 64 * ty
-            if m == 1 and ty == 1:
-                flat[at : at + 64, :] = jnp.zeros((64, 768), F32)
-                continue
-            src = 2 * ty if m == 0 else (6 if ty == 0 else 8)
-            flat[at : at + 64, 0:384] = brecv[src]
-            flat[at : at + 64, 384:768] = brecv[src + 1]
-        ks[256 * m : 256 * m + 256, :] = jnp.zeros((256, 768), F32)
-        for f in range(NF):
-            ks[256 * m + 8 * f : 256 * m + 8 * f + 6, :] = flat[6 * f : 6 * f + 6, :]
-    khi, klo = halves(ks[...])
-    low = low_lanes((256, 128))
-    for n in range(2):
-        qhi, qlo = halves(qs[256 * n : 256 * n + 256, :])
-        g = dot_nt(khi, qhi) + dot_nt(klo, qhi) + dot_nt(khi, qlo)
-        for j in range(2):
-            c, h = g[0:256, 128 * j : 128 * j + 128], g[256:512, 128 * j : 128 * j + 128]
-            esend[0, 2 * n + j] = jnp.where(low, c, swap(h))
-            esend[1, 2 * n + j] = jnp.where(low, swap(c), h)
+def early_gram(brecv, qs, qcat, flat, esend):
+    hi, lo = halves(qs[...])
+    qcat[...] = jnp.concatenate([hi, hi, lo], axis=1)
+    for i in range(5):
+        flat[64 * i : 64 * i + 64, 0:384] = brecv[2 * i]
+        flat[64 * i : 64 * i + 64, 384:768] = brecv[2 * i + 1]
+    hi, lo = halves(flat[...])
+    out = dot_nt(jnp.concatenate([hi, lo, hi], axis=1), qcat[...])
+    low = low_lanes((192, 128))
+    zero = jnp.zeros((64, 128), F32)
+    for n in range(4):
+        o = out[:, 128 * n : 128 * n + 128]
+        c, h = o[0:192], jnp.concatenate([o[192:256], zero, o[256:320]], axis=0)
+        esend[n // 2, 2 * (n % 2)] = jnp.where(low, c, swap(h))
+        esend[n // 2, 2 * (n % 2) + 1] = jnp.where(low, swap(c), h)
+
 
 def term(recv, res, hit, fourr, kinr, liver, vz, hres, hsend, z, zl_):
     his, los = [], []
@@ -489,39 +483,92 @@
 F0, F1 = 10, 22
 
 
-def late_gram(hrecv, qs, flat, ks, lsend):
-    ks[...] = jnp.zeros((96, 768), F32)
+def late_gram(hrecv, qcat, flat, lsend, start):
     flat[0:64, 0:384] = hrecv[0]
     flat[0:64, 384:768] = hrecv[1]
-    for f in range(F0, F1):
-        k0, k1 = max(6 * f, 64), min(6 * f + 6, 128)
-        o = 8 * (f - F0) + k0 - 6 * f
-        ks[o : o + k1 - k0, :] = flat[k0 - 64 : k1 - 64, :]
-    khi, klo = halves(ks[...])
-    low = low_lanes((48, 128))
-    for n in range(2):
-        qhi, qlo = halves(qs[256 * n : 256 * n + 256, :])
-        g = dot_nt(khi, qhi) + dot_nt(klo, qhi) + dot_nt(khi, qlo)
-        for j in range(2):
-            a, b = g[0:48, 128 * j : 128 * j + 128], g[48:96, 128 * j : 128 * j + 128]
-            lsend[0, 2 * n + j] = jnp.where(low, a, swap(b))
-            lsend[1, 2 * n + j] = jnp.where(low, swap(a), b)
-
-
-def step_kernel(ev, cur_h, hcur_h, prev_h, hprev_h, gm_h, scols_h, pot_h, wz_h, wy_h, wx_h, vx_h, vy_h,
+    hi, lo = halves(flat[0:64, :])
+    cat = jnp.concatenate([hi, lo, hi], axis=1)
+    low = low_lanes((32, 128))
+    mine = lax.rem(lax.axis_index("band"), 2)
+    for core in (1 - mine, mine):
+        out = dot_nt(cat, qcat[pl.ds(pl.multiple_of(256 * core, 256), 256), :])
+        for n in range(2):
+            a, b = out[0:32, 128 * n : 128 * n + 128], out[32:64, 128 * n : 128 * n + 128]
+            lsend[core, 2 * n] = jnp.where(low, a, swap(b))
+            lsend[core, 2 * n + 1] = jnp.where(low, swap(a), b)
+        if core is not mine:
+            start()
+
+
+def late_tiles(total, la, lb, fl):
+    other = swap(total)
+    la[8:40, :], la[40:72, :] = total, other
+    lb[8:40, :], lb[40:72, :] = other, total
+    low = low_lanes((3, 128))
+    for i in range(F1 - F0):
+        r = 8 + 6 * (F0 + i) - 64
+        fl[8 * i : 8 * i + 3, :] = jnp.where(low, la[r : r + 3, :], lb[r + 3 : r + 6, :])
+
+
+class LateExchange:
+    def __init__(self, src, dst, ssem, rsem):
+        self.a = (src, dst, ssem, rsem)
+        self.f = lax.axis_index("fft")
+        self.owner = jnp.logical_and(self.f >= F0, self.f < F1)
+
+    def start(self):
+        src, dst, ssem, rsem = self.a
+        f, b = self.f, lax.axis_index("band")
+        to_me = dst.at[pl.ds(pl.multiple_of(8 * f, 8), 4), :]
+        for i in range(F1 - F0):
+            n = lax.rem(f + i, F1 - F0)
+            part = src.at[pl.ds(pl.multiple_of(8 * n, 8), 4), :]
+
+            @pl.when(n + F0 != f)
+            def _():
+                pltpu.make_async_remote_copy(
+                    src_ref=part, dst_ref=to_me, send_sem=ssem, recv_sem=rsem, device_id=(b, n + F0),
+                    device_id_type=MESH).start()
+
+        @pl.when(self.owner)
+        def _():
+            own = src.at[pl.ds(pl.multiple_of(8 * (f - F0), 8), 4), :]
+            pltpu.make_async_copy(own, to_me, rsem).start()
+
+    def add(self, out, scale):
+        src, dst, ssem, rsem = self.a
+
+        @pl.when(self.owner)
+        def _():
+            whole(dst.at[pl.ds(0, 4 * NF), :], rsem)
+            total = dst[0:4, :]
+            for d in range(1, NF):
+                total = total + dst[8 * d : 8 * d + 4, :]
+            total = total[0:3] * scale
+            low = low_lanes((3, 128))
+            out[0:3, :] = out[0:3, :] + jnp.where(low, 0.0, swap(total))
+            out[3:6, :] = out[3:6, :] + jnp.where(low, 0.0, total)
+
+    def sent(self):
+        src, dst, ssem, rsem = self.a
+        whole(src.at[pl.ds(0, 44), :], ssem)
+        pl.when(jnp.logical_not(self.owner))(lambda: whole(src.at[pl.ds(0, 4), :], ssem))
+
+
+def step_kernel(ev_h, cur_h, hcur_h, prev_h, hprev_h, gm_h, scols_h, pot_h, wz_h, wy_h, wx_h, vx_h, vy_h,
                 vz_h, hres_h, out,
-                cur, hcur, prev, hprev, gm, scols, pot, wz, wy, wx, vx, vy, vz, hres,
+                ev, cur, hcur, prev, hprev, gm, scols, pot, wz, wy, wx, vx, vy, vz, hres,
                 res, kinr, gfour, liver, ghit, glhs, y, send, bsend,
                 recv, brecv, shit, smask, sfour, slhs, potp, pm, tt, gg, gl, send2, recv2,
-                qs, flat, ks, esend, egot, emid, erecv, z, zl, hsend, hrecv, lks,
-                lsend, lgot, lmid, lrecv, fsend, frecv, s1, r1, s3, r3, s4, s6, sems, load):
-    pairs = [(gm_h, gm), (scols_h, scols), (cur_h, cur), (hcur_h, hcur), (wz_h, wz), (prev_h, prev), (hprev_h, hprev),
+                qs, qcat, flat, esum, esend, egot, emid, erecv, z, zl, hsend, hrecv, la, lb,
+                lsend, lgot, lmid, lrecv, fl, lrow, fsend, frecv, s1, r1, s3, r3, s4, s6, sems, load):
+    pairs = [(ev_h, ev), (gm_h, gm), (scols_h, scols), (cur_h, cur), (hcur_h, hcur), (wz_h, wz), (prev_h, prev), (hprev_h, hprev),
              (pot_h, pot), (wy_h, wy), (wx_h, wx), (vx_h, vx), (vy_h, vy), (vz_h, vz)]
     loads = [pltpu.make_async_copy(a, b, load.at[i]) for i, (a, b) in enumerate(pairs)]
     for copy in loads:
         copy.start()
     greet_everyone()
-    for copy in loads[:5]:
+    for copy in loads[:6]:
         copy.wait()
     x1 = FftExchange(send, recv, s1, r1)
     x2 = BandExchange(bsend, brecv, band_rows, sems.at[0], sems.at[1])
@@ -529,20 +576,21 @@
     x4 = BandSum(esend, egot, emid, erecv, s4)
     x5 = BandExchange(hsend, hrecv, band_rows, sems.at[4], sems.at[5])
     x6 = BandSum(lsend, lgot, lmid, lrecv, s6)
+    x8 = LateExchange(fl, lrow, sems.at[6], sems.at[7])
     x7 = FftExchange(fsend, frecv, sems.at[pl.ds(8, 1)], sems.at[pl.ds(9, 1)])
     residual(ev, cur, hcur, gm, scols, res, glhs, ghit, kinr, gfour, liver)
     sticks(glhs, ghit, wz, send, y)
     everyone_in()
     for g in range(3):
         x1.start(g)
-    for copy in loads[5:]:
+    for copy in loads[6:]:
         copy.wait()
     basis_rows(cur, hcur, prev, hprev, res, liver, bsend)
+    x2.start()
     plane_maps(scols, pot, shit, smask, sfour, potp)
 
     def plane(g, carry):
         x1.wait(g)
-        pl.when(g == 0)(x2.start)
         place(g, recv, shit, smask, slhs, pm)
         along_y(pm, wy, tt)
         along_x(g, tt, potp, wx, vx, vy, gg)
@@ -553,7 +601,7 @@
     lax.fori_loop(0, 3, plane, 0)
     x2.wait()
     row_side(brecv, qs)
-    early_gram(brecv, qs, flat, ks, esend)
+    early_gram(brecv, qs, qcat, flat, esend)
     x4.first()
     x4.second()
     for g in range(3):
@@ -562,26 +610,31 @@
     x5.start()
     store = pltpu.make_async_copy(hres, hres_h, load.at[15])
     store.start()
-    fsend[...] = x4.total()
+    esum[...] = x4.total()
+    fsend[...] = jnp.zeros((256, 128), F32)
+    for f in range(NF):
+        fsend[8 * f : 8 * f + 6, :] = esum[6 * f : 6 * f + 6, :]
+    x7.start()
+    fl[...] = jnp.zeros((8 * (F1 - F0), 128), F32)
+    la[...] = jnp.zeros((80, 128), F32)
+    lb[...] = jnp.zeros((80, 128), F32)
     x5.wait()
-    late_gram(hrecv, qs, flat, lks, lsend)
-    x6.first()
+    late_gram(hrecv, qcat, flat, lsend, x6.first)
     x6.second()
-    low = low_lanes((48, 128))
-    total = x6.total()
-    fsend[8 * F0 : 8 * F0 + 48, :] = fsend[8 * F0 : 8 * F0 + 48, :] + jnp.where(low, 0.0, swap(total))
-    fsend[8 * F0 + 48 : 8 * F0 + 96, :] = fsend[8 * F0 + 48 : 8 * F0 + 96, :] + jnp.where(low, 0.0, total)
-    x7.start()
     x7.wait()
     total = frecv[0:8, :]
     for d in range(1, NF):
         total = total + frecv[8 * d : 8 * d + 8, :]
-    out[...] = total * (8.0 / float(L**3))
+    scale = 8.0 / float(L**3)
+    out[...] = total * scale
+    late_tiles(x6.total(), la, lb, fl)
+    x8.start()
+    x8.add(out, scale)
     store.wait()
     for g in range(3):
         x1.sent(g)
         x3.sent(g)
-    for x in (x2, x4, x5, x6, x7):
+    for x in (x2, x4, x5, x6, x7, x8):
         x.sent()
 
 
@@ -601,18 +654,19 @@
     v16 = lambda *shape: pltpu.VMEM(shape, BF16)
     vi = lambda *shape: pltpu.VMEM(shape, jnp.int32)
     hres, tile = pl.pallas_call(
-        step_kernel, out_shape=(sds(2, 8, 3072), sds(8, 128)), in_specs=[SM] + [HB] * 13, out_specs=(HB, VM),
+        step_kernel, out_shape=(sds(2, 8, 3072), sds(8, 128)), in_specs=[HB] * 14, out_specs=(HB, VM),
         scratch_shapes=[
-            vm(2, 8, 3072), vm(2, 8, 3072), vm(2, 8, 3072), vm(2, 8, 3072), vi(1, 3072), vi(NF, 128), vm(3, L, L),
+            pltpu.SMEM((8,), F32), vm(2, 8, 3072), vm(2, 8, 3072), vm(2, 8, 3072), vm(2, 8, 3072), vi(1, 3072), vi(NF, 128), vm(3, L, L),
             v16(384, 192), v16(384, 256), v16(192, 336), v16(112, 576), v16(256, 256), v16(128, 288),
             vm(2, 8, 3072),
             vm(16, 3072), vm(8, 3072), vi(8, 3072), vm(8, 3072), v16(256, 3072), v16(416, 3072), vm(512, 128),
             vm(768, 128), vm(8, 10, 8, 384),
             vm(768, 128), vm(10, 64, 384), v16(256, 2048), v16(208, 2048), vi(8, 2048), v16(416, 2048),
             vm(3, L, 128), vm(416, 128), vm(2, 448, 128), vm(448, 128), v16(208, 512), vm(768, 128), vm(768, 128),
-            vm(512, 768), vm(192, 768), vm(512, 768), vm(2, 4, 256, 128), vm(4, 256, 128), vm(4, 256, 128),
-            vm(4, 256, 128), vm(512, 128),
-            v16(208, 512), vm(8, 2, 8, 384), vm(2, 64, 384), vm(96, 768), vm(2, 4, 48, 128), vm(4, 48, 128), vm(4, 48, 128), vm(4, 48, 128),
+            vm(512, 768), v16(512, 2304), vm(320, 768), vm(192, 128), vm(2, 4, 192, 128), vm(4, 192, 128), vm(4, 192, 128),
+            vm(4, 192, 128), vm(512, 128),
+            v16(208, 512), vm(8, 2, 8, 384), vm(2, 64, 384), vm(80, 128), vm(80, 128), vm(2, 4, 32, 128), vm(4, 32, 128), vm(4, 32, 128),
+            vm(4, 32, 128), vm(96, 128), vm(256, 128),
             vm(256, 128), vm(256, 128), DMA((3,)), DMA((3,)), DMA((3,)), DMA((3,)), DMA((4,)), DMA((4,)), DMA((10,)), DMA((16,))],
         compiler_params=pltpu.CompilerParams(collective_id=0, has_side_effects=True, vmem_limit_bytes=BIG), name="step",
     )(eigen_values, current, h_current, previous, h_previous, gm, sc, potential,

time: 59.3 us -> 54.7 us (0.922)
  the two profiles are of different devices: /device:TPU:8 before, /device:TPU:4 now
where the time goes in v4:
time: 54.7 us; the launch traced here: 54.6 us
  Pallas kernels  50.9 us (93%)
  local copies, waits for them, and re-layouts  2.98 us (5%)
  between operations  0.65 us (1%)
    pallas_call x1, Pallas kernels, local(): pl.pallas_call(step_kernel, out_shape=(sds(2, 8, 3072), sds(8, 128)), in_...  50.9 us
    unnamed x3, local copies, waits for them, and re-layouts  2.29 us

profile of v4, /device:TPU:4, one launch (start us, length us, event | category | flops | bytes accessed | tf_op | source)
XLA Modules:
  0.0 54.6 jit_solution(700092298762073751)
XLA Ops:
  0.6 50.9 %step.1 = (f32[2,8,3072]{2,1,0:T(8,128)}, f32[8,128]{1,0:T(8,128)}) custom-call(f32[8]{0:T(128)} %ev_h.1, f32[2,8,3072]{2,1,0:T(8,128)} %cur_h.1, f32[2,8,3072]{2,1,0:T(8,128)} %hcur_h.1, f32[2,8,3072]{2,1,0:T(8,128)} %prev_h.1, f32[2,8,3072]{2,1,0:T(8,128)} %hprev_h.1, s32[1,3072]{1,0:T(1,128)} %bitcast.6, s32[32,128]{1,0:T(8,128)} %bitcast.5, ...), custom_call_target="tpu_custom_call" | custom-call | tf_op jit(solution)/shard_map/step/pallas_call | solution.py:656
  51.6 0.0 copy-start
  51.6 0.7 %copy-done = f32[8,128]{1,0:T(8,128)S(1)} copy-done((f32[8,128]{1,0:T(8,128)S(1)}, f32[8,128]{1,0:T(8,128)}, u32[]{:S(2)}) %copy-start) | copy-done | bytes 4120
  52.2 0.1 reshape.17
  52.3 0.6 %fusion = (f32[2,24,6]{1,0,2:T(2,128)}, f32[2,24,6]{1,0,2:T(2,128)}) fusion(f32[4,24,6]{1,0,2:T(4,128)S(1)} %slice_bitcast_fusion), kind=kLoop, calls=%fused_computation.1 | loop fusion | bytes 4608 | tf_op jit(solution)/shard_map/slice | solution.py:675
  52.9 1.6 %copy.18 = f32[2,8,3072]{2,1,0:T(8,128)} copy(f32[2,8,3072]{2,1,0:T(8,128)} %get-tuple-element.12) | data formatting | bytes 393216
  (1 shorter events, 0.0 us)
Async XLA Ops:
  51.6 0.7 %copy-start = (f32[8,128]{1,0:T(8,128)S(1)}, f32[8,128]{1,0:T(8,128)}, u32[]{:S(2)}) copy-start(f32[8,128]{1,0:T(8,128)} %get-tuple-element.6) | copy-start | bytes 12292

commit v5 on v4

--- a/solution.py
+++ b/solution.py
@@ -244,7 +244,7 @@
 
     def wait(self, g=0):
         src, dst, ssem, rsem = self.a
-        whole(dst.at[pl.ds(pl.multiple_of(256 * g, 256), 256), :], rsem.at[g])
+        whole(dst.at[pl.ds(256 * g, 256), :], rsem.at[g])
 
     def sent(self, g=0):
         src, dst, ssem, rsem = self.a
@@ -336,7 +336,7 @@
     low = low_lanes((8, 128))
     for k in range(16):
         at = pl.ds(128 * k, 128)
-        base = pl.multiple_of(256 * g + 16 * k, 16)
+        base = 256 * g + 16 * k
         r0, r1 = recv[pl.ds(base, 8), :], recv[pl.ds(base + 8, 8), :]
         hi, lo = halves(jnp.concatenate([jnp.where(low, r0, swap(r1)), jnp.where(low, swap(r0), r1)], axis=0))
         for t in range(NT):
@@ -415,7 +415,7 @@
         acc = pick(gl[...], hit, fourr, n, 256)
         for k in range(2):
             re, im = acc[0:8, 128 * k : 128 * k + 128], acc[8:16, 128 * k : 128 * k + 128]
-            base = pl.multiple_of(256 * g + 32 * n + 16 * k, 16)
+            base = 256 * g + 32 * n + 16 * k
             send[pl.ds(base, 8), :] = jnp.where(low, re, swap(im))
             send[pl.ds(base + 8, 8), :] = jnp.where(low, swap(re), im)
 
@@ -559,13 +559,13 @@
                 vz_h, hres_h, out,
                 ev, cur, hcur, prev, hprev, gm, scols, pot, wz, wy, wx, vx, vy, vz, hres,
                 res, kinr, gfour, liver, ghit, glhs, y, send, bsend,
-                recv, brecv, shit, smask, sfour, slhs, potp, pm, tt, gg, gl, send2, recv2,
+                recv, brecv, shit, smask, sfour, slhs, potp, pm, pm2, tt, gg, gl, send2, recv2,
                 qs, qcat, flat, esum, esend, egot, emid, erecv, z, zl, hsend, hrecv, la, lb,
                 lsend, lgot, lmid, lrecv, fl, lrow, fsend, frecv, s1, r1, s3, r3, s4, s6, sems, load):
     pairs = [(ev_h, ev), (gm_h, gm), (scols_h, scols), (cur_h, cur), (hcur_h, hcur), (wz_h, wz), (prev_h, prev), (hprev_h, hprev),
              (pot_h, pot), (wy_h, wy), (wx_h, wx), (vx_h, vx), (vy_h, vy), (vz_h, vz)]
     loads = [pltpu.make_async_copy(a, b, load.at[i]) for i, (a, b) in enumerate(pairs)]
-    for copy in loads:
+    for copy in loads[:6]:
         copy.start()
     greet_everyone()
     for copy in loads[:6]:
@@ -579,26 +579,31 @@
     x8 = LateExchange(fl, lrow, sems.at[6], sems.at[7])
     x7 = FftExchange(fsend, frecv, sems.at[pl.ds(8, 1)], sems.at[pl.ds(9, 1)])
     residual(ev, cur, hcur, gm, scols, res, glhs, ghit, kinr, gfour, liver)
+    for copy in loads[6:]:
+        copy.start()
     sticks(glhs, ghit, wz, send, y)
     everyone_in()
-    for g in range(3):
-        x1.start(g)
+    x1.start(0)
     for copy in loads[6:]:
         copy.wait()
     basis_rows(cur, hcur, prev, hprev, res, liver, bsend)
+    x1.start(1)
+    plane_maps(scols, pot, shit, smask, sfour, potp)
+    x1.start(2)
     x2.start()
-    plane_maps(scols, pot, shit, smask, sfour, potp)
-
-    def plane(g, carry):
-        x1.wait(g)
-        place(g, recv, shit, smask, slhs, pm)
-        along_y(pm, wy, tt)
+
+    pms = (pm, pm2)
+    x1.wait(0)
+    place(0, recv, shit, smask, slhs, pms[0])
+    for g in range(3):
+        if g < 2:
+            x1.wait(g + 1)
+        along_y(pms[g % 2], wy, tt)
+        if g < 2:
+            place(g + 1, recv, shit, smask, slhs, pms[(g + 1) % 2])
         along_x(g, tt, potp, wx, vx, vy, gg)
         collect(g, gg, shit, sfour, gl, send2)
         x3.start(g)
-        return carry
-
-    lax.fori_loop(0, 3, plane, 0)
     x2.wait()
     row_side(brecv, qs)
     early_gram(brecv, qs, qcat, flat, esend)
@@ -662,7 +667,7 @@
             vm(16, 3072), vm(8, 3072), vi(8, 3072), vm(8, 3072), v16(256, 3072), v16(416, 3072), vm(512, 128),
             vm(768, 128), vm(8, 10, 8, 384),
             vm(768, 128), vm(10, 64, 384), v16(256, 2048), v16(208, 2048), vi(8, 2048), v16(416, 2048),
-            vm(3, L, 128), vm(416, 128), vm(2, 448, 128), vm(448, 128), v16(208, 512), vm(768, 128), vm(768, 128),
+            vm(3, L, 128), vm(416, 128), vm(416, 128), vm(2, 448, 128), vm(448, 128), v16(208, 512), vm(768, 128), vm(768, 128),
             vm(512, 768), v16(512, 2304), vm(320, 768), vm(192, 128), vm(2, 4, 192, 128), vm(4, 192, 128), vm(4, 192, 128),
             vm(4, 192, 128), vm(512, 128),
             v16(208, 512), vm(8, 2, 8, 384), vm(2, 64, 384), vm(80, 128), vm(80, 128), vm(2, 4, 32, 128), vm(4, 32, 128), vm(4, 32, 128),

time: 54.7 us -> 53.8 us (0.984)
  Pallas kernels: 50.9 us -> 50 us
    pallas_call x1, Pallas kernels: 50.9 us -> 50 us  [local(): pl.pallas_call(step_kernel, out_shape=(sds(2, 8, 3072), sds(8, 128)), in_...]
where the time goes in v5:
time: 53.8 us; the launch traced here: 53.7 us
  Pallas kernels  50 us (93%)
  local copies, waits for them, and re-layouts  2.98 us (6%)
  between operations  0.65 us (1%)
    pallas_call x1, Pallas kernels, local(): pl.pallas_call(step_kernel, out_shape=(sds(2, 8, 3072), sds(8, 128)), in_...  50 us
    unnamed x3, local copies, waits for them, and re-layouts  2.29 us

profile of v5, /device:TPU:4, one launch (start us, length us, event | category | flops | bytes accessed | tf_op | source)
XLA Modules:
  0.0 53.7 jit_solution(4277817739810512372)
XLA Ops:
  0.6 50.0 %step.1 = (f32[2,8,3072]{2,1,0:T(8,128)}, f32[8,128]{1,0:T(8,128)}) custom-call(f32[8]{0:T(128)} %ev_h.1, f32[2,8,3072]{2,1,0:T(8,128)} %cur_h.1, f32[2,8,3072]{2,1,0:T(8,128)} %hcur_h.1, f32[2,8,3072]{2,1,0:T(8,128)} %prev_h.1, f32[2,8,3072]{2,1,0:T(8,128)} %hprev_h.1, s32[1,3072]{1,0:T(1,128)} %bitcast.6, s32[32,128]{1,0:T(8,128)} %bitcast.5, ...), custom_call_target="tpu_custom_call" | custom-call | tf_op jit(solution)/shard_map/step/pallas_call | solution.py:661
  50.7 0.0 copy-start
  50.7 0.7 %copy-done = f32[8,128]{1,0:T(8,128)S(1)} copy-done((f32[8,128]{1,0:T(8,128)S(1)}, f32[8,128]{1,0:T(8,128)}, u32[]{:S(2)}) %copy-start) | copy-done | bytes 4120
  51.4 0.1 reshape.17
  51.4 0.6 %fusion = (f32[2,24,6]{1,0,2:T(2,128)}, f32[2,24,6]{1,0,2:T(2,128)}) fusion(f32[4,24,6]{1,0,2:T(4,128)S(1)} %slice_bitcast_fusion), kind=kLoop, calls=%fused_computation.1 | loop fusion | bytes 4608 | tf_op jit(solution)/shard_map/slice | solution.py:680
  52.0 1.6 %copy.18 = f32[2,8,3072]{2,1,0:T(8,128)} copy(f32[2,8,3072]{2,1,0:T(8,128)} %get-tuple-element.12) | data formatting | bytes 393216
  (1 shorter events, 0.0 us)
Async XLA Ops:
  50.7 0.7 %copy-start = (f32[8,128]{1,0:T(8,128)S(1)}, f32[8,128]{1,0:T(8,128)}, u32[]{:S(2)}) copy-start(f32[8,128]{1,0:T(8,128)} %get-tuple-element.6) | copy-start | bytes 12292

commit v6 on v5

--- a/solution.py
+++ b/solution.py
@@ -308,6 +308,33 @@
         whole(mid.at[pl.ds(0, 3)], sems.at[2])
 
 
+class LateSum:
+    def __init__(self, src, dst, sems):
+        self.a = (src, dst, sems)
+
+    def start(self, core, mine):
+        src, dst, sems = self.a
+        f, b = lax.axis_index("fft"), lax.axis_index("band")
+        y = b // 2
+        for i in (2, 1, 3, 0):
+            to = lax.rem(y + i, 4)
+            if mine and i == 0:
+                pltpu.make_async_copy(src.at[core, to], dst.at[b], sems.at[1]).start()
+            else:
+                pltpu.make_async_remote_copy(
+                    src_ref=src.at[core, to], dst_ref=dst.at[b], send_sem=sems.at[0], recv_sem=sems.at[1],
+                    device_id=(2 * to + core, f), device_id_type=MESH).start()
+
+    def total(self):
+        src, dst, sems = self.a
+        whole(dst, sems.at[1])
+        return ((dst[0] + dst[1]) + (dst[2] + dst[3])) + ((dst[4] + dst[5]) + (dst[6] + dst[7]))
+
+    def sent(self):
+        src, dst, sems = self.a
+        whole(dst.at[pl.ds(0, NBD - 1)], sems.at[0])
+
+
 def band_rows(dst, frm):
     return dst.at[:, pl.ds(pl.multiple_of(frm * 8, 8), 8), :]
 
@@ -496,8 +523,7 @@
             a, b = out[0:32, 128 * n : 128 * n + 128], out[32:64, 128 * n : 128 * n + 128]
             lsend[core, 2 * n] = jnp.where(low, a, swap(b))
             lsend[core, 2 * n + 1] = jnp.where(low, swap(a), b)
-        if core is not mine:
-            start()
+        start(core, core is mine)
 
 
 def late_tiles(total, la, lb, fl):
@@ -544,10 +570,9 @@
             total = dst[0:4, :]
             for d in range(1, NF):
                 total = total + dst[8 * d : 8 * d + 4, :]
-            total = total[0:3] * scale
-            low = low_lanes((3, 128))
-            out[0:3, :] = out[0:3, :] + jnp.where(low, 0.0, swap(total))
-            out[3:6, :] = out[3:6, :] + jnp.where(low, 0.0, total)
+            total = total * scale
+            both = jnp.concatenate([swap(total)[0:3], total[0:3], jnp.zeros((2, 128), F32)], axis=0)
+            out[...] = out[...] + jnp.where(low_lanes((8, 128)), 0.0, both)
 
     def sent(self):
         src, dst, ssem, rsem = self.a
@@ -561,8 +586,8 @@
                 res, kinr, gfour, liver, ghit, glhs, y, send, bsend,
                 recv, brecv, shit, smask, sfour, slhs, potp, pm, pm2, tt, gg, gl, send2, recv2,
                 qs, qcat, flat, esum, esend, egot, emid, erecv, z, zl, hsend, hrecv, la, lb,
-                lsend, lgot, lmid, lrecv, fl, lrow, fsend, frecv, s1, r1, s3, r3, s4, s6, sems, load):
-    pairs = [(ev_h, ev), (gm_h, gm), (scols_h, scols), (cur_h, cur), (hcur_h, hcur), (wz_h, wz), (prev_h, prev), (hprev_h, hprev),
+                lsend, lrecv, fl, lrow, fsend, frecv, s1, r1, s3, r3, s4, s6, sems, load):
+    pairs = [(ev_h, ev), (gm_h, gm), (scols_h, scols.at[pl.ds(0, NF), :]), (cur_h, cur), (hcur_h, hcur), (wz_h, wz), (prev_h, prev), (hprev_h, hprev),
              (pot_h, pot), (wy_h, wy), (wx_h, wx), (vx_h, vx), (vy_h, vy), (vz_h, vz)]
     loads = [pltpu.make_async_copy(a, b, load.at[i]) for i, (a, b) in enumerate(pairs)]
     for copy in loads[:6]:
@@ -575,7 +600,7 @@
     x3 = FftExchange(send2, recv2, s3, r3)
     x4 = BandSum(esend, egot, emid, erecv, s4)
     x5 = BandExchange(hsend, hrecv, band_rows, sems.at[4], sems.at[5])
-    x6 = BandSum(lsend, lgot, lmid, lrecv, s6)
+    x6 = LateSum(lsend, lrecv, s6)
     x8 = LateExchange(fl, lrow, sems.at[6], sems.at[7])
     x7 = FftExchange(fsend, frecv, sems.at[pl.ds(8, 1)], sems.at[pl.ds(9, 1)])
     residual(ev, cur, hcur, gm, scols, res, glhs, ghit, kinr, gfour, liver)
@@ -615,17 +640,16 @@
     x5.start()
     store = pltpu.make_async_copy(hres, hres_h, load.at[15])
     store.start()
-    esum[...] = x4.total()
+    esum[0:192, :] = x4.total()
     fsend[...] = jnp.zeros((256, 128), F32)
     for f in range(NF):
         fsend[8 * f : 8 * f + 6, :] = esum[6 * f : 6 * f + 6, :]
     x7.start()
     fl[...] = jnp.zeros((8 * (F1 - F0), 128), F32)
-    la[...] = jnp.zeros((80, 128), F32)
-    lb[...] = jnp.zeros((80, 128), F32)
+    la[...] = jnp.zeros((88, 128), F32)
+    lb[...] = jnp.zeros((88, 128), F32)
     x5.wait()
-    late_gram(hrecv, qcat, flat, lsend, x6.first)
-    x6.second()
+    late_gram(hrecv, qcat, flat, lsend, x6.start)
     x7.wait()
     total = frecv[0:8, :]
     for d in range(1, NF):
@@ -661,17 +685,16 @@
     hres, tile = pl.pallas_call(
         step_kernel, out_shape=(sds(2, 8, 3072), sds(8, 128)), in_specs=[HB] * 14, out_specs=(HB, VM),
         scratch_shapes=[
-            pltpu.SMEM((8,), F32), vm(2, 8, 3072), vm(2, 8, 3072), vm(2, 8, 3072), vm(2, 8, 3072), vi(1, 3072), vi(NF, 128), vm(3, L, L),
+            pltpu.SMEM((8,), F32), vm(2, 8, 3072), vm(2, 8, 3072), vm(2, 8, 3072), vm(2, 8, 3072), vi(1, 3072), vi(NF + 8, 128), vm(3, L, L),
             v16(384, 192), v16(384, 256), v16(192, 336), v16(112, 576), v16(256, 256), v16(128, 288),
             vm(2, 8, 3072),
             vm(16, 3072), vm(8, 3072), vi(8, 3072), vm(8, 3072), v16(256, 3072), v16(416, 3072), vm(512, 128),
             vm(768, 128), vm(8, 10, 8, 384),
             vm(768, 128), vm(10, 64, 384), v16(256, 2048), v16(208, 2048), vi(8, 2048), v16(416, 2048),
             vm(3, L, 128), vm(416, 128), vm(416, 128), vm(2, 448, 128), vm(448, 128), v16(208, 512), vm(768, 128), vm(768, 128),
-            vm(512, 768), v16(512, 2304), vm(320, 768), vm(192, 128), vm(2, 4, 192, 128), vm(4, 192, 128), vm(4, 192, 128),
+            vm(512, 768), v16(512, 2304), vm(320, 768), vm(200, 128), vm(2, 4, 192, 128), vm(4, 192, 128), vm(4, 192, 128),
             vm(4, 192, 128), vm(512, 128),
-            v16(208, 512), vm(8, 2, 8, 384), vm(2, 64, 384), vm(80, 128), vm(80, 128), vm(2, 4, 32, 128), vm(4, 32, 128), vm(4, 32, 128),
-            vm(4, 32, 128), vm(96, 128), vm(256, 128),
+            v16(208, 512), vm(8, 2, 8, 384), vm(2, 64, 384), vm(88, 128), vm(88, 128), vm(2, 4, 32, 128), vm(8, 32, 128), vm(96, 128), vm(256, 128),
             vm(256, 128), vm(256, 128), DMA((3,)), DMA((3,)), DMA((3,)), DMA((3,)), DMA((4,)), DMA((4,)), DMA((10,)), DMA((16,))],
         compiler_params=pltpu.CompilerParams(collective_id=0, has_side_effects=True, vmem_limit_bytes=BIG), name="step",
     )(eigen_values, current, h_current, previous, h_previous, gm, sc, potential,

time: 53.8 us -> 53.6 us (level)
  no operation moved by 1% of the time
where the time goes in v6:
time: 53.6 us; the launch traced here: 53.4 us
  Pallas kernels  49.8 us (93%)
  local copies, waits for them, and re-layouts  2.98 us (6%)
  between operations  0.65 us (1%)
    pallas_call x1, Pallas kernels, local(): pl.pallas_call(step_kernel, out_shape=(sds(2, 8, 3072), sds(8, 128)), in_...  49.8 us
    unnamed x3, local copies, waits for them, and re-layouts  2.29 us

profile of v6, /device:TPU:4, one launch (start us, length us, event | category | flops | bytes accessed | tf_op | source)
XLA Modules:
  0.0 53.4 jit_solution(17541493589166489361)
XLA Ops:
  0.6 49.8 %step.1 = (f32[2,8,3072]{2,1,0:T(8,128)}, f32[8,128]{1,0:T(8,128)}) custom-call(f32[8]{0:T(128)} %ev_h.1, f32[2,8,3072]{2,1,0:T(8,128)} %cur_h.1, f32[2,8,3072]{2,1,0:T(8,128)} %hcur_h.1, f32[2,8,3072]{2,1,0:T(8,128)} %prev_h.1, f32[2,8,3072]{2,1,0:T(8,128)} %hprev_h.1, s32[1,3072]{1,0:T(1,128)} %bitcast.6, s32[32,128]{1,0:T(8,128)} %bitcast.5, ...), custom_call_target="tpu_custom_call" | custom-call | tf_op jit(solution)/shard_map/step/pallas_call | solution.py:685
  50.4 0.0 copy-start
  50.4 0.7 %copy-done = f32[8,128]{1,0:T(8,128)S(1)} copy-done((f32[8,128]{1,0:T(8,128)S(1)}, f32[8,128]{1,0:T(8,128)}, u32[]{:S(2)}) %copy-start) | copy-done | bytes 4120
  51.1 0.1 reshape.17
  51.2 0.6 %fusion = (f32[2,24,6]{1,0,2:T(2,128)}, f32[2,24,6]{1,0,2:T(2,128)}) fusion(f32[4,24,6]{1,0,2:T(4,128)S(1)} %slice_bitcast_fusion), kind=kLoop, calls=%fused_computation.1 | loop fusion | bytes 4608 | tf_op jit(solution)/shard_map/slice | solution.py:703
  51.8 1.6 %copy.18 = f32[2,8,3072]{2,1,0:T(8,128)} copy(f32[2,8,3072]{2,1,0:T(8,128)} %get-tuple-element.12) | data formatting | bytes 393216
  (1 shorter events, 0.0 us)
Async XLA Ops:
  50.4 0.7 %copy-start = (f32[8,128]{1,0:T(8,128)S(1)}, f32[8,128]{1,0:T(8,128)}, u32[]{:S(2)}) copy-start(f32[8,128]{1,0:T(8,128)} %get-tuple-element.6) | copy-start | bytes 12292

commit v7 on v6

--- a/solution.py
+++ b/solution.py
@@ -510,10 +510,8 @@
 F0, F1 = 10, 22
 
 
-def late_gram(hrecv, qcat, flat, lsend, start):
-    flat[0:64, 0:384] = hrecv[0]
-    flat[0:64, 384:768] = hrecv[1]
-    hi, lo = halves(flat[0:64, :])
+def late_gram(hrecv, qcat, lsend, start):
+    hi, lo = halves(jnp.concatenate([hrecv[0], hrecv[1]], axis=1))
     cat = jnp.concatenate([hi, lo, hi], axis=1)
     low = low_lanes((32, 128))
     mine = lax.rem(lax.axis_index("band"), 2)
@@ -567,10 +565,10 @@
         @pl.when(self.owner)
         def _():
             whole(dst.at[pl.ds(0, 4 * NF), :], rsem)
-            total = dst[0:4, :]
-            for d in range(1, NF):
-                total = total + dst[8 * d : 8 * d + 4, :]
-            total = total * scale
+            parts = [dst[8 * d : 8 * d + 4, :] for d in range(NF)]
+            while len(parts) > 1:
+                parts = [a + b for a, b in zip(parts[::2], parts[1::2])]
+            total = parts[0] * scale
             both = jnp.concatenate([swap(total)[0:3], total[0:3], jnp.zeros((2, 128), F32)], axis=0)
             out[...] = out[...] + jnp.where(low_lanes((8, 128)), 0.0, both)
 
@@ -649,7 +647,7 @@
     la[...] = jnp.zeros((88, 128), F32)
     lb[...] = jnp.zeros((88, 128), F32)
     x5.wait()
-    late_gram(hrecv, qcat, flat, lsend, x6.start)
+    late_gram(hrecv, qcat, lsend, x6.start)
     x7.wait()
     total = frecv[0:8, :]
     for d in range(1, NF):

time: 53.6 us -> 53.6 us (level)
  no operation moved by 1% of the time
where the time goes in v7:
time: 53.6 us; the launch traced here: 53.4 us
  Pallas kernels  49.7 us (93%)
  local copies, waits for them, and re-layouts  2.98 us (6%)
  between operations  0.65 us (1%)
    pallas_call x1, Pallas kernels, local(): pl.pallas_call(step_kernel, out_shape=(sds(2, 8, 3072), sds(8, 128)), in_...  49.7 us
    unnamed x3, local copies, waits for them, and re-layouts  2.29 us

profile of v7, /device:TPU:4, one launch (start us, length us, event | category | flops | bytes accessed | tf_op | source)
XLA Modules:
  0.0 53.4 jit_solution(14201000592224304579)
XLA Ops:
  0.6 49.7 %step.1 = (f32[2,8,3072]{2,1,0:T(8,128)}, f32[8,128]{1,0:T(8,128)}) custom-call(f32[8]{0:T(128)} %ev_h.1, f32[2,8,3072]{2,1,0:T(8,128)} %cur_h.1, f32[2,8,3072]{2,1,0:T(8,128)} %hcur_h.1, f32[2,8,3072]{2,1,0:T(8,128)} %prev_h.1, f32[2,8,3072]{2,1,0:T(8,128)} %hprev_h.1, s32[1,3072]{1,0:T(1,128)} %bitcast.6, s32[32,128]{1,0:T(8,128)} %bitcast.5, ...), custom_call_target="tpu_custom_call" | custom-call | tf_op jit(solution)/shard_map/step/pallas_call | solution.py:683
  50.4 0.0 copy-start
  50.4 0.7 %copy-done = f32[8,128]{1,0:T(8,128)S(1)} copy-done((f32[8,128]{1,0:T(8,128)S(1)}, f32[8,128]{1,0:T(8,128)}, u32[]{:S(2)}) %copy-start) | copy-done | bytes 4120
  51.1 0.1 reshape.17
  51.1 0.6 %fusion = (f32[2,24,6]{1,0,2:T(2,128)}, f32[2,24,6]{1,0,2:T(2,128)}) fusion(f32[4,24,6]{1,0,2:T(4,128)S(1)} %slice_bitcast_fusion), kind=kLoop, calls=%fused_computation.1 | loop fusion | bytes 4608 | tf_op jit(solution)/shard_map/slice | solution.py:701
  51.8 1.6 %copy.18 = f32[2,8,3072]{2,1,0:T(8,128)} copy(f32[2,8,3072]{2,1,0:T(8,128)} %get-tuple-element.12) | data formatting | bytes 393216
  (1 shorter events, 0.0 us)
Async XLA Ops:
  50.4 0.7 %copy-start = (f32[8,128]{1,0:T(8,128)S(1)}, f32[8,128]{1,0:T(8,128)}, u32[]{:S(2)}) copy-start(f32[8,128]{1,0:T(8,128)} %get-tuple-element.6) | copy-start | bytes 12292
